TPU v7x, 512 devices: a whole 4x4x16 slice. The times are simulated.
512 devices in a mesh: seq: 8 (over y, core), tp: 16 (over z), dp: 4 (over x).
Axes of the slice: x: 4, y: 4, z: 16, core: 2. Of those that a mesh axis runs over, the one named last changes fastest.
Arguments:
- query_rows: bfloat16 [4, 1024, 8192], P('dp', 'seq', 'tp'), may hold values from -8 to 8
- key_rows: bfloat16 [4, 1024, 1024], P('dp', 'seq', 'tp'), may hold values from -6 to 6
- value_rows: bfloat16 [4, 1024, 1024], P('dp', 'seq', 'tp'), may hold values from -6 to 6
- gate_rows: bfloat16 [4, 1024, 8192], P('dp', 'seq', 'tp'), may hold values from -6 to 6
- write_vec: bfloat16 [4, 1024, 128], P('dp', 'seq'), may hold values from -0.5 to 0.5
- read_vec: bfloat16 [4, 1024, 128], P('dp', 'seq'), may hold values from -0.5 to 0.5
- dt_raw: float32 [4, 128, 1024], P('dp', 'tp', 'seq'), may hold values from -4 to 4
- a_log: float32 [128], P('tp')
- skip_gain: float32 [128], P('tp'), may hold values from 0.5 to 1.5
- dt_bias: float32 [128], P('tp'), may hold values from -1 to 1
- out_grad: bfloat16 [4, 1024, 8192], P('dp', 'seq', 'tp'), may hold values from -6 to 6
Outputs:
- grad_query: float32 [4, 1024, 8192], P('dp', 'seq', 'tp')
- grad_key: float32 [4, 1024, 1024], P('dp', 'seq', 'tp')
- grad_value: float32 [4, 1024, 1024], P('dp', 'seq', 'tp')
- grad_gate: float32 [4, 1024, 8192], P('dp', 'seq', 'tp')
- grad_write: float32 [4, 1024, 128], P('dp', 'seq')
- grad_read: float32 [4, 1024, 128], P('dp', 'seq')
- grad_dt: float32 [4, 128, 1024], P('dp', 'tp', 'seq')
- grad_alog: float32 [128], P('tp')
- grad_skip: float32 [128], P('tp')
- grad_bias: float32 [128], P('tp')
All inputs are finite; a program needn't handle non-finite values.
Results may differ from a plain program's by a relative error of at most 0.024.
Values may be sent and summed in bfloat16 or wider, within the bound.
A program may use at most 64 MiB of HBM per device.

v0:
```python
import math

import jax
import jax.numpy as jnp
from jax import lax
from jax.sharding import PartitionSpec as P

NEG_FILL = -1e30
HIGH = lax.Precision.HIGHEST


def from_partner(array, axis, distance):
    return lax.ppermute(array, axis, [(i, i ^ 1 << distance) for i in range(lax.axis_size(axis))])


def carried_in(array, axis, join, neutral):
    place = lax.axis_index(axis)
    gathered = jax.tree.map(
        lambda a, kind: lax.all_gather(a.astype(kind), axis), array, (jnp.bfloat16, jnp.bfloat16)
    )
    state = jax.tree.map(lambda a, e: jnp.zeros_like(a) + jnp.asarray(e, a.dtype), array, neutral)

    def one(turn, state):
        return join(
            state,
            jax.tree.map(
                lambda a, own: lax.dynamic_index_in_dim(a, turn, 0, False).astype(own.dtype),
                gathered,
                array,
            ),
        )

    return lax.fori_loop(0, place, one, state)


def prefix(array, axis, combine, identity):
    devices, here = (lax.axis_size(axis), lax.axis_index(axis))
    everything = jax.tree.map(lambda part: lax.all_gather(part, axis), array)
    start = jax.tree.map(
        lambda part, zero: jnp.broadcast_to(jnp.asarray(zero, part.dtype), part.shape),
        array,
        identity,
    )

    def turn(k, before):
        at = devices - 1 - k
        reached = at > here
        new = combine(before, jax.tree.map(lambda part: part[at], everything))
        return jax.tree.map(lambda a, b: jnp.where(reached, a, b), new, before)

    return lax.fori_loop(0, devices, turn, start)


def block_scan(inner, gate_in, write_in, read_in, dt_raw, a_log, skip_gain, dt_bias):
    num_rows, num_heads, head_width = inner.shape
    num_states = write_in.shape[1]
    block_len = math.gcd(num_rows, 256)
    block_count = num_rows // block_len
    step_dt = jax.nn.softplus(dt_raw + dt_bias[:, None])
    rate_all = step_dt * jnp.exp(a_log)[:, None]
    rate_blocks = rate_all.reshape(num_heads, block_count, block_len).transpose(1, 0, 2)
    dt_blocks = step_dt.reshape(num_heads, block_count, block_len).transpose(1, 0, 2)
    inner_blocks = inner.reshape(block_count, block_len, num_heads, head_width)
    write_blocks = write_in.reshape(block_count, block_len, num_states)
    read_blocks = read_in.reshape(block_count, block_len, num_states)
    causal = jnp.arange(block_len)[:, None] >= jnp.arange(block_len)[None, :]

    def advance(carried, pieces):
        rate_now, dt_now, inner_now, write_now, read_now = pieces
        cum_rate = jnp.cumsum(rate_now, axis=1)
        intersection = jnp.dot(read_now, write_now.T, precision=HIGH)
        log_gap = cum_rate[:, :, None] - cum_rate[:, None, :]
        weight = (
            jnp.where(causal, jnp.exp(-jnp.maximum(log_gap, 0.0)), 0.0)
            * intersection[None]
            * dt_now[:, None, :]
        )
        output = jnp.einsum("hts,shp->thp", weight, inner_now, precision=HIGH)
        output = (
            output
            + jnp.einsum("tn,hpn->thp", read_now, carried, precision=HIGH)
            * jnp.exp(-cum_rate).T[:, :, None]
        )
        to_end = jnp.exp(-(cum_rate[:, -1:] - cum_rate)) * dt_now
        next_state = jnp.exp(-cum_rate[:, -1])[:, None, None] * carried + jnp.einsum(
            "hs,shp,sn->hpn", to_end, inner_now, write_now, precision=HIGH
        )
        return (next_state, output)

    zero_state = jnp.zeros((num_heads, head_width, num_states), jnp.float32)
    end_state, outputs = lax.scan(
        advance, zero_state, (rate_blocks, dt_blocks, inner_blocks, write_blocks, read_blocks)
    )
    mixed_out = outputs.reshape(num_rows, num_heads, head_width) + skip_gain[None, :, None] * inner
    gated_out = mixed_out.reshape(num_rows, num_heads * head_width) * jax.nn.silu(gate_in)
    return (gated_out, end_state, jnp.exp(-jnp.sum(rate_all, axis=1)))


def entry_term(gate_in, read_in, dt_raw, a_log, dt_bias, entry_state):
    step_dt = jax.nn.softplus(dt_raw + dt_bias[:, None])
    cum_rate = jnp.cumsum(step_dt * jnp.exp(a_log)[:, None], axis=1)
    carried = (
        jnp.einsum("tn,hpn->thp", read_in, entry_state, precision=HIGH)
        * jnp.exp(-cum_rate).T[:, :, None]
    )
    return carried.reshape(read_in.shape[0], -1) * jax.nn.silu(gate_in)


def carry_combine(earlier, later):
    return (earlier[0] * later[0], later[0][:, None, None] * earlier[1] + later[1])


def join_halves(own_part, other_part, parity):
    lower_first = jnp.concatenate([own_part, other_part], axis=1)
    upper_first = jnp.concatenate([other_part, own_part], axis=1)
    return jnp.where(parity == 0, lower_first, upper_first)


def block_scores(query_blk, key_piece, key_start, row_pos, scale):
    scores = (
        jnp.einsum("rhd,kd->hrk", query_blk, key_piece, preferred_element_type=jnp.float32) * scale
    )
    allowed = (key_start + jnp.arange(key_piece.shape[0]))[None, :] <= row_pos[:, None]
    return jnp.where(allowed[None], scores, NEG_FILL)


def attend_forward(query_blk, full_keys, full_values, first_row):
    num_rows, num_heads, head_dim = query_blk.shape
    key_block = math.gcd(full_keys.shape[0], 512)
    scale = head_dim ** (-0.5)
    row_pos = first_row + jnp.arange(num_rows)
    needed = (first_row + num_rows + key_block - 1) // key_block

    def visit(index, carry):
        run_max, run_sum, run_acc = carry
        key_start = index * key_block
        key_piece = lax.dynamic_slice_in_dim(full_keys, key_start, key_block, 0)
        value_piece = lax.dynamic_slice_in_dim(full_values, key_start, key_block, 0)
        scores = block_scores(query_blk, key_piece, key_start, row_pos, scale)
        new_max = jnp.maximum(run_max, jnp.max(scores, axis=2))
        shrink = jnp.exp(run_max - new_max)
        probs = jnp.exp(scores - new_max[:, :, None])
        run_sum = run_sum * shrink + jnp.sum(probs, axis=2)
        update = jnp.einsum(
            "hrk,kd->hrd",
            probs.astype(jnp.bfloat16),
            value_piece,
            preferred_element_type=jnp.float32,
        )
        run_acc = run_acc * shrink[:, :, None] + update
        return (new_max, run_sum, run_acc)

    start_max = jnp.full((num_heads, num_rows), NEG_FILL, jnp.float32)
    start_sum = jnp.zeros((num_heads, num_rows), jnp.float32)
    start_acc = jnp.zeros((num_heads, num_rows, head_dim), jnp.float32)
    run_max, run_sum, run_acc = lax.fori_loop(0, needed, visit, (start_max, start_sum, start_acc))
    return (run_acc / run_sum[:, :, None], run_max + jnp.log(run_sum))


def attend_backward(query_blk, full_keys, full_values, first_row, attn, log_sum, grad_attn):
    num_rows, num_heads, head_dim = query_blk.shape
    seq_len = full_keys.shape[0]
    key_block = math.gcd(seq_len, 512)
    scale = head_dim ** (-0.5)
    row_pos = first_row + jnp.arange(num_rows)
    needed = (first_row + num_rows + key_block - 1) // key_block
    delta = jnp.sum(grad_attn * attn, axis=2)
    grad_low = grad_attn.astype(jnp.bfloat16)

    def visit(index, carry):
        grad_q, key_terms, value_terms = carry
        key_start = index * key_block
        key_piece = lax.dynamic_slice_in_dim(full_keys, key_start, key_block, 0)
        value_piece = lax.dynamic_slice_in_dim(full_values, key_start, key_block, 0)
        scores = block_scores(query_blk, key_piece, key_start, row_pos, scale)
        probs = jnp.exp(scores - log_sum[:, :, None])
        probs_low = probs.astype(jnp.bfloat16)
        value_part = jnp.einsum(
            "hrk,hrd->kd", probs_low, grad_low, preferred_element_type=jnp.float32
        )
        grad_probs = jnp.einsum(
            "hrd,kd->hrk", grad_low, value_piece, preferred_element_type=jnp.float32
        )
        grad_scores = (probs * (grad_probs - delta[:, :, None])).astype(jnp.bfloat16)
        grad_q = grad_q + jnp.einsum(
            "hrk,kd->rhd", grad_scores, key_piece, preferred_element_type=jnp.float32
        )
        key_part = (
            jnp.einsum("hrk,rhd->kd", grad_scores, query_blk, preferred_element_type=jnp.float32)
            * scale
        )
        key_terms = lax.dynamic_update_slice_in_dim(key_terms, key_part, key_start, 0)
        value_terms = lax.dynamic_update_slice_in_dim(value_terms, value_part, key_start, 0)
        return (grad_q, key_terms, value_terms)

    start_q = jnp.zeros((num_rows, num_heads, head_dim), jnp.float32)
    start_terms = jnp.zeros((seq_len, head_dim), jnp.float32)
    grad_q, key_terms, value_terms = lax.fori_loop(
        0, needed, visit, (start_q, start_terms, start_terms)
    )
    return (grad_q * scale, key_terms, value_terms)


def body(
    query_rows,
    key_rows,
    value_rows,
    gate_rows,
    write_vec,
    read_vec,
    dt_raw,
    a_log,
    skip_gain,
    dt_bias,
    out_grad,
):
    num_rows = query_rows.shape[1]
    half_dim = key_rows.shape[2]
    head_dim = 2 * half_dim
    query_blk = query_rows[0].reshape(num_rows, -1, head_dim)
    parity = lax.axis_index("tp") % 2
    first_row = lax.axis_index("seq") * num_rows
    other_keys, other_values = from_partner((key_rows[0], value_rows[0]), "tp", 0)
    local_keys = join_halves(key_rows[0], other_keys, parity)
    local_values = join_halves(value_rows[0], other_values, parity)
    full_keys, full_values = (
        lax.all_gather(local_keys, "seq", axis=0, tiled=True),
        lax.all_gather(local_values, "seq", axis=0, tiled=True),
    )
    attn, log_sum = attend_forward(query_blk, full_keys, full_values, first_row)
    mamba_heads = a_log.shape[0]
    inner_heads = attn.transpose(1, 0, 2).reshape(num_rows, mamba_heads, -1)
    gate_f = gate_rows[0].astype(jnp.float32)
    write_f = write_vec[0].astype(jnp.float32)
    read_f = read_vec[0].astype(jnp.float32)
    raw_dt = dt_raw[0]
    main_outs, main_pullback = jax.vjp(
        block_scan, inner_heads, gate_f, write_f, read_f, raw_dt, a_log, skip_gain, dt_bias
    )
    local_state = main_outs[1]
    local_decay = main_outs[2]
    identity = (jnp.ones_like(local_decay), jnp.zeros_like(local_state))
    entry_state = carried_in((local_decay, local_state), "seq", carry_combine, identity)[1]
    cotangent = out_grad[0].astype(jnp.float32)
    entry_out, entry_pullback = jax.vjp(
        entry_term, gate_f, read_f, raw_dt, a_log, dt_bias, entry_state
    )
    entry_gate, entry_read, entry_dt, entry_alog, entry_bias, entry_grad = entry_pullback(cotangent)
    exit_grad = prefix((local_decay, entry_grad), "seq", carry_combine, identity)[1]
    decay_grad = jnp.sum(exit_grad * entry_state, axis=(1, 2))
    main_grads = main_pullback((cotangent, exit_grad, decay_grad))
    main_inner, main_gate, main_write, main_read, main_dt, main_alog, main_skip, main_bias = (
        main_grads
    )
    grad_write, grad_read = (
        lax.psum(main_write.astype(jnp.bfloat16), "tp").astype(jnp.float32),
        lax.psum((main_read + entry_read).astype(jnp.bfloat16), "tp").astype(jnp.float32),
    )
    grad_alog, grad_skip, grad_bias = lax.psum(
        (main_alog + entry_alog, main_skip, main_bias + entry_bias), ("seq", "dp")
    )
    grad_attn = main_inner.reshape(num_rows, -1, head_dim).transpose(1, 0, 2)
    grad_q, key_terms, value_terms = attend_backward(
        query_blk, full_keys, full_values, first_row, attn, log_sum, grad_attn
    )
    own_start = parity * half_dim
    give_start = (1 - parity) * half_dim
    key_sum, value_sum = (
        lax.psum_scatter(
            key_terms.astype(jnp.bfloat16), "seq", scatter_dimension=0, tiled=True
        ).astype(jnp.float32),
        lax.psum_scatter(
            value_terms.astype(jnp.bfloat16), "seq", scatter_dimension=0, tiled=True
        ).astype(jnp.float32),
    )
    give_key = lax.dynamic_slice_in_dim(key_sum, give_start, half_dim, 1)
    give_value = lax.dynamic_slice_in_dim(value_sum, give_start, half_dim, 1)
    received = (
        from_partner(give_key.astype(jnp.bfloat16), "tp", 0).astype(give_key.dtype),
        from_partner(give_value.astype(jnp.bfloat16), "tp", 0).astype(give_value.dtype),
    )
    grad_key = lax.dynamic_slice_in_dim(key_sum, own_start, half_dim, 1) + received[0]
    grad_value = lax.dynamic_slice_in_dim(value_sum, own_start, half_dim, 1) + received[1]
    grad_query = grad_q.reshape(num_rows, -1)[None]
    grad_gate = (main_gate + entry_gate)[None]
    grad_dt = (main_dt + entry_dt)[None]
    return (
        grad_query,
        grad_key[None],
        grad_value[None],
        grad_gate,
        grad_write[None],
        grad_read[None],
        grad_dt,
        grad_alog,
        grad_skip,
        grad_bias,
    )


def solution(mesh):
    in_specs = (
        P("dp", "seq", "tp"),
        P("dp", "seq", "tp"),
        P("dp", "seq", "tp"),
        P("dp", "seq", "tp"),
        P("dp", "seq", None),
        P("dp", "seq", None),
        P("dp", "tp", "seq"),
        P("tp"),
        P("tp"),
        P("tp"),
        P("dp", "seq", "tp"),
    )
    out_specs = (
        P("dp", "seq", "tp"),
        P("dp", "seq", "tp"),
        P("dp", "seq", "tp"),
        P("dp", "seq", "tp"),
        P("dp", "seq", None),
        P("dp", "seq", None),
        P("dp", "tp", "seq"),
        P("tp"),
        P("tp"),
        P("tp"),
    )
    return jax.shard_map(body, mesh=mesh, in_specs=in_specs, out_specs=out_specs, check_vma=False)
```

profile of v0, /device:TPU:1, one launch (start us, length us, event | category | flops | bytes accessed | tf_op | source)
XLA Modules:
  0.0 367.2 jit_solution(5791027247772604833)
XLA Ops:
  8.1 4.4 %collective-permute-start = (bf16[128,64]{1,0:T(8,128)(2,1)S(1)}, bf16[128,64]{1,0:T(8,128)(2,1)S(1)}, u32[]{:S(2)}, u32[]{:S(2)}) collective-permute-start(bf16[128,64]{1,0:T(8,128)(2,1)S(1)} %bitcast.298), channel_id=1, source_target_pairs={{0,4},{4,0},{8,12},{12,8},{16,20},{20,16},{24,28},{28,24},{32,36},... | collective-permute-start | bytes 49160 | tf_op jit(solution)/shard_map/ppermute | solution.py:13
  13.3 1.9 collective-permute-start.1
  21.7 19.1 %all_gather.26 = bf16[1024,128]{1,0:T(8,128)(2,1)S(1)} all-gather(bf16[128,128]{1,0:T(8,128)(2,1)S(1)} %maximum_select_fusion), channel_id=1, replica_groups=mesh['seq'=8,'tp'=16,'dp'=4] {'seq'}, dimensions={0}, use_global_device_ids=true | all-gather | bytes 294912 | tf_op jit(solution)/shard_map/all_gather | solution.py:227
  40.9 12.8 %all_gather.27 = bf16[1024,128]{1,0:T(8,128)(2,1)S(1)} all-gather(bf16[128,128]{1,0:T(8,128)(2,1)S(1)} %maximum_select_fusion.1), channel_id=1, replica_groups=mesh['seq'=8,'tp'=16,'dp'=4] {'seq'}, dimensions={0}, use_global_device_ids=true | all-gather | bytes 294912 | tf_op jit(solution)/shard_map/all_gather | solution.py:228
  56.2 1.3 dynamic-slice.18
  58.5 11.9 %all-reduce.3 = bf16[64]{0:T(256)(128)(2,1)S(1)} all-reduce(bf16[64]{0:T(256)(128)(2,1)S(1)} %dynamic-update-slice.1), channel_id=5, replica_groups=mesh['seq'=8,'tp'=16,'dp'=4] {'seq'}, use_global_device_ids=true, to_apply=%add.3 | all-reduce | flops 64 | bytes 256
  71.1 1.9 fusion.37
  73.1 14.5 %all-gather.9.cloned.1.call-done = bf16[64,64,128]{2,1,0:T(8,128)(2,1)} async-done(((bf16[8,64,128]{2,1,0:T(8,128)(2,1)}), bf16[64,64,128]{2,1,0:T(8,128)(2,1)}) %all-gather.9.cloned.1.call-update) | async-done | bytes 1048592 | tf_op jit(solution)/shard_map/all_gather | solution.py:19
  88.9 1.2 fusion.72
  91.3 16.5 %all-reduce.2 = f32[64]{0:T(128)S(1)} all-reduce(f32[64]{0:T(128)S(1)} %get-tuple-element.744), channel_id=2, replica_groups=mesh['seq'=8,'tp'=16,'dp'=4] {'seq'}, use_global_device_ids=true, to_apply=%add.2 | all-reduce | flops 64 | bytes 512
  110.3 1.4 fusion.127
  112.5 17.1 %all-gather.7.cloned.1.call-done = f32[64,64,128]{2,1,0:T(8,128)} async-done(((f32[8,64,128]{2,1,0:T(8,128)}), f32[64,64,128]{2,1,0:T(8,128)}) %all-gather.7.cloned.1.call-update) | async-done | bytes 2097168 | tf_op jit(solution)/shard_map/all_gather | solution.py:38
  129.6 8.8 %while.19 = (s32[]{:T(128)}, f32[8,64,128]{2,1,0:T(8,128)S(1)}, s32[]{:T(128)}, f32[8,8]{1,0:T(8,128)S(1)}, f32[8,8,64,128]{3,2,1,0:T(8,128)}, /*index=5*/s32[]{:T(128)}, s32[]{:T(128)}, s32[]{:T(128)}, s32[]{:T(128)}) while((s32[]{:T(128)}, f32[8,64,128]{2,1,0:T(8,128)S(1)}, s32[]{:T(128)}, f32[8,8]{1,0:T(8,128)S(1)}, ...), condition=%wide.region_7.9_spmd.clone, body=%wide.region_6.8_spmd.clone.sunk | while | flops 262152 | bytes 786695 | solution.py:51
  142.1 2.1 while.18
  146.2 1.2 reduce_window_sum.34
  149.0 64.1 %all-reduce.4 = (f32[8]{0:T(128)}, f32[8]{0:T(128)}, f32[8]{0:T(128)}) all-reduce(f32[8]{0:T(128)S(1)} %add_multiply_fusion.1, f32[8]{0:T(128)S(1)} %reduce_sum.239, f32[8]{0:T(128)S(1)} %add.247), channel_id=1, replica_groups=mesh['seq'=8,'tp'=16,'dp'=4] {'seq','dp'}, use_global_device_ids=true, to_apply=%region_30.32 | all-reduce | flops 24 | bytes 192 | tf_op jit(solution)/shard_map/psum | solution.py:259
  214.6 54.2 %all-reduce.8.cloned.1.call-done = (bf16[1,128,128]{2,1,0:T(8,128)(2,1)}, bf16[1,128,128]{2,1,0:T(8,128)(2,1)}) async-done(((bf16[1,128,128]{2,1,0:T(8,128)(2,1)}, bf16[1,128,128]{2,1,0:T(8,128)(2,1)}), (bf16[1,128,128]{2,1,0:T(8,128)(2,1)}, bf16[1,128,128]{2,1,0:T(8,128)(2,1)})) %all-reduce.8.cloned.1.call-update) | async-done | bytes 65552 | tf_op jit(solution)/shard_map/psum | solution.py:256
  268.8 1.4 broadcast_in_dim.183
  270.2 1.4 broadcast_in_dim.185
  271.6 43.3 %reduce-scatter.9.cloned.1.call-done = bf16[128,128]{1,0:T(8,128)(2,1)} async-done(((bf16[1024,128]{1,0:T(8,128)(2,1)}), bf16[128,128]{1,0:T(8,128)(2,1)}) %reduce-scatter.9.cloned.1.call-update) | async-done | bytes 32784
  315.9 2.3 collective-permute-start.3
  318.1 36.5 %reduce-scatter.7.cloned.1.call-done = bf16[128,128]{1,0:T(8,128)(2,1)} async-done(((bf16[1024,128]{1,0:T(8,128)(2,1)}), bf16[128,128]{1,0:T(8,128)(2,1)}) %reduce-scatter.7.cloned.1.call-update) | async-done | bytes 32784
  355.6 2.3 collective-permute-start.2
  358.5 1.6 collective-permute-done.2
  (148 shorter events, 41.4 us)
Async XLA Ops:
  7.2 63.5 %copy-start = (bf16[1,128,128]{2,1,0:T(8,128)(2,1)S(1)}, bf16[1,128,128]{2,1,0:T(8,128)(2,1)}, u32[]{:S(2)}) copy-start(bf16[1,128,128]{2,1,0:T(8,128)(2,1)} %param.25) | copy-start | bytes 98308
  7.2 80.3 %all-gather.9.cloned.1.call-start = ((), (), s32[]{:S(2)}) async-start(), calls=%async_computation.3 | async-start | bytes 1179648 | tf_op jit(solution)/shard_map/all_gather | solution.py:19
  8.1 13.6 %collective-permute-start = (bf16[128,64]{1,0:T(8,128)(2,1)S(1)}, bf16[128,64]{1,0:T(8,128)(2,1)S(1)}, u32[]{:S(2)}, u32[]{:S(2)}) collective-permute-start(bf16[128,64]{1,0:T(8,128)(2,1)S(1)} %bitcast.298), channel_id=1, source_target_pairs={{0,4},{4,0},{8,12},{12,8},{16,20},{20,16},{24,28},{28,24},{32,36},... | collective-permute-start | bytes 49160 | tf_op jit(solution)/shard_map/ppermute | solution.py:13
  13.3 27.6 %collective-permute-start.1 = (bf16[128,64]{1,0:T(8,128)(2,1)S(1)}, bf16[128,64]{1,0:T(8,128)(2,1)S(1)}, u32[]{:S(2)}, u32[]{:S(2)}) collective-permute-start(bf16[128,64]{1,0:T(8,128)(2,1)S(1)} %bitcast.296), channel_id=1, source_target_pairs={{0,4},{4,0},{8,12},{12,8},{16,20},{20,16},{24,28},{28,24},{32,36},... | collective-permute-start | bytes 49160 | tf_op jit(solution)/shard_map/ppermute | solution.py:13
  53.8 1.4 copy-start.1
  54.9 15.6 %copy-start.4 = (f32[8]{0:T(128)S(1)}, f32[8]{0:T(128)}, u32[]{:S(2)}) copy-start(f32[8]{0:T(128)} %param.28) | copy-start | bytes 100
  56.2 73.4 %all-gather.7.cloned.1.call-start = ((), (), s32[]{:S(2)}) async-start(), calls=%async_computation.2 | async-start | bytes 2359296 | tf_op jit(solution)/shard_map/all_gather | solution.py:38
  91.1 177.7 %all-reduce.8.cloned.1.call-start = ((), (), s32[]{:S(2)}) async-start(), calls=%async_computation.6 | async-start | bytes 131072 | tf_op jit(solution)/shard_map/psum | solution.py:256
  139.1 1.8 copy-start.2
  139.2 1.8 copy-start.3
  142.1 6.9 %copy-start.5 = (f32[8]{0:T(128)S(1)}, f32[8]{0:T(128)}, u32[]{:S(2)}) copy-start(f32[8]{0:T(128)} %param.27) | copy-start | bytes 100
  144.2 170.8 %reduce-scatter.9.cloned.1.call-start = ((), (), s32[]{:S(2)}) async-start(), calls=%async_computation.5 | async-start | bytes 294912
  145.2 209.4 %reduce-scatter.7.cloned.1.call-start = ((), (), s32[]{:S(2)}) async-start(), calls=%async_computation.4 | async-start | bytes 294912
  315.9 42.0 %collective-permute-start.3 = (bf16[128,64]{0,1:T(8,128)(2,1)S(1)}, bf16[128,64]{0,1:T(8,128)(2,1)S(1)}, u32[]{:S(2)}, u32[]{:S(2)}) collective-permute-start(bf16[128,64]{0,1:T(8,128)(2,1)S(1)} %dynamic-slice_convert_fusion), channel_id=1, source_target_pairs={{0,4},{4,0},{8,12},{12,8},{16,20},{20,16},{24,28},{28,24},{32,36},... | collective-permute-start | bytes 49160 | tf_op jit(solution)/shard_map/ppermute | solution.py:13
  355.6 4.5 %collective-permute-start.2 = (bf16[128,64]{0,1:T(8,128)(2,1)S(1)}, bf16[128,64]{0,1:T(8,128)(2,1)S(1)}, u32[]{:S(2)}, u32[]{:S(2)}) collective-permute-start(bf16[128,64]{0,1:T(8,128)(2,1)S(1)} %dynamic-slice_convert_fusion.1), channel_id=1, source_target_pairs={{0,4},{4,0},{8,12},{12,8},{16,20},{20,16},{24,28},{28,24},{32,36},... | collective-permute-start | bytes 49160 | tf_op jit(solution)/shard_map/ppermute | solution.py:13
Sparse Core Ops, SparseCore 0:
  56.3 31.1 all-gather.8
  91.3 38.2 all-gather.6
  144.3 124.4 all-reduce.7
  271.7 43.1 reduce-scatter.8
  317.6 37.0 reduce-scatter.6
where the time goes:
time: 370 us; the launch traced here: 367 us
  waiting for transfers between devices  167 us (45%)
  blocking collectives  124 us (34%)
  other arithmetic  22.2 us (6%)
  between operations  14.9 us (4%)
  local copies, waits for them, and re-layouts  13.9 us (4%)
  matrix products  12.7 us (3%)
  starting transfers between devices  11 us (3%)
    unnamed x7, waiting for transfers between devices  79.9 us
    psum x1, blocking collectives, body(): lax.psum((main_alog + entry_alog, main_skip, main_bias + entry_bias), ('s...  64.1 us
    psum x1, waiting for transfers between devices, body(): lax.psum(main_write.astype(jnp.bfloat16), 'tp').astype(jnp.float32)  54.2 us
    unnamed x2, blocking collectives  28.4 us
    all_gather x1, blocking collectives, body(): lax.all_gather(local_keys, 'seq', axis=0, tiled=True)  19.1 us
    all_gather x1, waiting for transfers between devices, prefix(): everything = jax.tree.map(lambda part: lax.all_gather(part, axis), array)  17.1 us
    all_gather x1, waiting for transfers between devices, carried_in(): lax.all_gather(a.astype(kind), axis)  14.5 us
    all_gather x1, blocking collectives, body(): lax.all_gather(local_values, 'seq', axis=0, tiled=True)  12.8 us
  transfers between devices with their start and end apart: 9, of which 6 were waited for; matrix products, arithmetic and copies ran while one was open for 7% of the time, Pallas kernels for 0%

commit v1 on v0

v1 whole, which is shorter than its diff:
```python
import functools

import jax
import jax.numpy as jnp
from jax import lax
from jax.experimental import pallas as pl
from jax.experimental.pallas import tpu as pltpu
from jax.sharding import PartitionSpec as P

HIGH = lax.Precision.HIGHEST
MESH = pl.DeviceIdType.MESH
F32 = jnp.float32
BF16 = jnp.bfloat16
NEG_FILL = -1e30


def mm(a, b, precision=None):
    return lax.dot_general(a, b, (((1,), (0,)), ((), ())), precision=precision, preferred_element_type=F32)


def mm_nt(a, b, precision=None):
    return lax.dot_general(a, b, (((1,), (1,)), ((), ())), precision=precision, preferred_element_type=F32)


def mm_tn(a, b, precision=None):
    return lax.dot_general(a, b, (((0,), (0,)), ((), ())), precision=precision, preferred_element_type=F32)


def kernel(
    dims,
    q_hbm, k_hbm, v_hbm, gate_hbm, write_hbm, read_hbm, dt_hbm, cot_hbm,
    alog_s, skip_s, bias_s,
    gq_hbm, gk_hbm, gv_hbm, gg_hbm, gw_hbm, gr_hbm, gdt_hbm, galog_s, gskip_s, gbias_s,
    q_v, k_v, v_v, gate_v, write_v, read_v, dt_v, cot_v,
    kv_buf, kf, vf, q_st, s_buf, m_buf, l_buf, acc, gl_st, delta_b,
    gy, dsc, ecx, w2x, dx, x_v, dtl_b, w_b, gym_b,
    cl_all, es_send, es_recv, es_out, ex_recv, fs_send, fs_recv, fs_out, fi_recv,
    kg_send, kg_recv, ps_send, ps_recv, ps_out, pp_all, pd_all, pf, pp_smem,
    gq_o, gk_o, gv_o, gg_o, gw_o, gr_o, gdt_o,
    in_sem, out_sem, kv_ss, kv_rs, cl_ss, cl_rs, es_ss, es_rs, ex_ss, ex_rs, fs_ss, fs_rs, fi_ss, fi_rs,
    kg_ss, kg_rs, p1_ss, p1_rs, p2_ss, p2_rs, pa_ss, pa_rs, pb_ss, pb_rs, sm_sem,
):
    nseq, ntp, ndp, nheads, nq = dims
    rows = 128
    s = lax.axis_index("seq")
    z = lax.axis_index("tp")
    x = lax.axis_index("dp")
    par = lax.rem(z, 2)
    base = z - par
    other = base + 1 - par
    chunk = lax.div(s, 2)
    scale = 128 ** (-0.5)

    def rcopy(src, dst, ssem, rsem, **where):
        return pltpu.make_async_remote_copy(
            src_ref=src, dst_ref=dst, send_sem=ssem, recv_sem=rsem, device_id=where, device_id_type=MESH
        )

    def seq_block(ref, i, n):
        return ref.at[pl.ds(pl.multiple_of(i * n, n), n)]

    loads = []
    for at, (src, dst) in enumerate((
        (k_hbm.at[0], k_v), (v_hbm.at[0], v_v), (dt_hbm.at[0], dt_v), (gate_hbm.at[0], gate_v),
        (cot_hbm.at[0], cot_v), (read_hbm.at[0], read_v), (write_hbm.at[0], write_v), (q_hbm.at[0], q_v),
    )):
        copy = pltpu.make_async_copy(src, dst, in_sem.at[at])
        copy.start()
        loads.append(copy)

    barrier = pltpu.get_barrier_semaphore()
    for d in range(1, nseq):
        to = lax.rem(s + d, nseq)
        pl.semaphore_signal(barrier, inc=1, device_id={"seq": to, "tp": z}, device_id_type=MESH)
        pl.semaphore_signal(barrier, inc=1, device_id={"seq": to, "tp": other}, device_id_type=MESH)
    for d in range(1, ntp):
        pl.semaphore_signal(barrier, inc=1, device_id={"tp": lax.rem(z + d, ntp)}, device_id_type=MESH)
    for d in range(1, ndp):
        pl.semaphore_signal(barrier, inc=1, device_id={"dp": lax.rem(x + d, ndp)}, device_id_type=MESH)

    loads[0].wait()
    loads[1].wait()
    own_rows = pl.ds(pl.multiple_of(s * rows, rows), rows)
    kv_buf[par, own_rows, :] = jnp.concatenate([k_v[...], v_v[...]], axis=1)

    @pl.when(lax.rem(s, 2) == 0)
    def _():
        blank = pl.ds(pl.multiple_of((s + 1) * rows, rows), rows)
        kv_buf[0, blank, :] = jnp.zeros((rows, 128), BF16)
        kv_buf[1, blank, :] = jnp.zeros((rows, 128), BF16)

    pl.semaphore_wait(barrier, 2 * (nseq - 1) + (ntp - 1) + (ndp - 1))

    def kv_copy(d, p, to_seq, to_tp):
        here = kv_buf.at[par, own_rows]
        return rcopy(here, here, kv_ss.at[d, p], kv_rs.at[par, s], seq=to_seq, tp=to_tp)

    kv_copy(0, 0, s, other).start()
    for d in range(1, nseq):
        @pl.when(s + d < nseq)
        def _(d=d):
            kv_copy(d, 0, s + d, base).start()
            kv_copy(d, 1, s + d, base + 1).start()

    row_i = lax.broadcasted_iota(jnp.int32, (rows, rows), 0)
    col_i = lax.broadcasted_iota(jnp.int32, (rows, rows), 1)
    causal = row_i >= col_i
    head_i = lax.broadcasted_iota(jnp.int32, (nheads, rows), 0)

    def head_rows(ref):
        out = jnp.zeros((nheads, rows), F32)
        for h in range(nheads):
            out = jnp.where(head_i == h, ref[h], out)
        return out

    wide = nheads * 64
    eb64 = jnp.where(
        lax.broadcasted_iota(jnp.int32, (nheads, wide), 1) // 64
        == lax.broadcasted_iota(jnp.int32, (nheads, wide), 0), 1.0, 0.0,
    ).astype(F32)
    eb128 = jnp.where(
        lax.broadcasted_iota(jnp.int32, (nheads, nheads * 128), 1) // 128
        == lax.broadcasted_iota(jnp.int32, (nheads, nheads * 128), 0), 1.0, 0.0,
    ).astype(F32)

    loads[2].wait()
    zdt = dt_v[...] + head_rows(bias_s)
    dt = jnp.maximum(zdt, 0.0) + jnp.log1p(jnp.exp(-jnp.abs(zdt)))
    sig_z = 1.0 / (1.0 + jnp.exp(-zdt))
    ea = jnp.exp(head_rows(alog_s))
    rate = dt * ea
    cum = mm(rate, jnp.where(row_i <= col_i, 1.0, 0.0).astype(F32), HIGH)
    cum_last = jnp.broadcast_to(cum[:, rows - 1:rows], (nheads, rows))
    cl_all[s] = cum_last

    def cl_copy(d, to):
        return rcopy(cl_all.at[s], cl_all.at[s], cl_ss.at[d], cl_rs.at[s], seq=to)

    for d in range(1, nseq):
        cl_copy(d, lax.rem(s + d, nseq)).start()

    ecum = jnp.exp(-cum)
    w2 = dt * jnp.exp(-(cum_last - cum))
    ecx[...] = mm_tn(ecum, eb64, HIGH)
    w2x[...] = mm_tn(w2, eb64, HIGH)
    cum_b = mm_tn(cum, eb128, HIGH)

    loads[3].wait()
    loads[4].wait()
    gate = gate_v[...].astype(F32)
    cot = cot_v[...].astype(F32)
    sig = 1.0 / (1.0 + jnp.exp(-gate))
    gy[...] = cot * gate * sig
    dsc[...] = cot * sig * (1.0 + gate * (1.0 - sig))
    loads[5].wait()
    gye = (gy[...] * ecx[...]).astype(BF16)
    es_send[...] = mm_tn(gye, read_v[...]).astype(BF16)

    def all_to_all(send, recv, ss, rs):
        def copy(d):
            to = lax.rem(s + d, nseq)
            return rcopy(seq_block(send, to, 64), recv.at[s], ss.at[d], rs.at[s], seq=to)
        for d in range(1, nseq):
            copy(d).start()
        recv[s] = send[pl.ds(pl.multiple_of(s * 64, 64), 64), :]
        return copy

    es_copy = all_to_all(es_send, es_recv, es_ss, es_rs)

    loads[6].wait()
    cb = mm_nt(read_v[...], write_v[...])
    lane_lo = lax.broadcasted_iota(jnp.int32, (rows, 128), 1) < 64
    skip_row = jnp.zeros((1, wide), F32)
    lane_head = lax.broadcasted_iota(jnp.int32, (1, wide), 1) // 64
    for h in range(nheads):
        skip_row = jnp.where(lane_head == h, skip_s[h], skip_row)
    for p in range(nheads // 2):
        lanes = slice(128 * p, 128 * p + 128)
        ws = []
        for c in range(2):
            h = 2 * p + c
            gap = cum_b[:, 128 * h:128 * h + 128] - cum[h:h + 1, :]
            dtl = jnp.where(causal, jnp.exp(-jnp.maximum(gap, 0.0)), 0.0) * dt[h:h + 1, :]
            dtl_b[p, 128 * c:128 * c + 128, :] = dtl
            ws.append((dtl * cb).astype(BF16))
        gp = gy[:, lanes]
        gym = jnp.concatenate([jnp.where(lane_lo, gp, 0.0), jnp.where(lane_lo, 0.0, gp)], axis=0).astype(BF16)
        gym_b[p] = gym
        w_b[p] = jnp.concatenate(ws, axis=1)
        dx[:, lanes] = mm_tn(jnp.concatenate(ws, axis=0), gym) + skip_row[:, lanes] * gp

    def wait_from(make, skip_self=True):
        for d in range(1, nseq):
            make(lax.rem(s + d, nseq)).wait_recv()

    wait_from(lambda j: rcopy(cl_all.at[j], cl_all.at[j], cl_ss.at[0], cl_rs.at[j], seq=j))
    wait_from(lambda j: rcopy(es_recv.at[j], es_recv.at[j], es_ss.at[0], es_rs.at[j], seq=j))

    def back_copy(out, recv, ss, rs, i):
        here = seq_block(recv, s, 64)
        return rcopy(out.at[i], here, ss.at[i], rs.at[s], seq=i)

    own_head = pl.ds(pl.multiple_of(s * 64, 64), 64)

    def send_back(out, recv, ss, rs, i):
        @pl.when(s != i)
        def _():
            back_copy(out, recv, ss, rs, i).start()

        @pl.when(s == i)
        def _():
            recv[own_head, :] = out[i]

    state = jnp.zeros((64, 128), F32)
    for i in reversed(range(nseq)):
        es_out[i] = state.astype(BF16)
        send_back(es_out, ex_recv, ex_ss, ex_rs, i)
        state = es_recv[i].astype(F32) + jnp.exp(-cl_all[i, pl.ds(s, 1), :]) * state

    loads[7].wait()
    for p in range(nq):
        q_st[128 * p:128 * p + 128, :] = q_v[:, 128 * p:128 * p + 128]
    m_buf[...] = jnp.full((nq * rows, 128), NEG_FILL, F32)
    l_buf[...] = jnp.zeros((nq * rows, 128), F32)
    acc[...] = jnp.zeros((nq * rows, 128), F32)

    def scores(i, carry):
        here = pl.ds(pl.multiple_of(i * 256, 256), 256)
        for c in range(2):
            j = 2 * i + c
            for p in range(2):
                @pl.when(jnp.logical_and(j <= s, jnp.logical_or(j != s, p != par)))
                def _(p=p, j=j):
                    slot = kv_buf.at[p, pl.ds(pl.multiple_of(j * rows, rows), rows)]
                    rcopy(slot, slot, kv_ss.at[0, 0], kv_rs.at[p, j], tp=other).wait_recv()
        kv0 = kv_buf[0, here, :]
        kv1 = kv_buf[1, here, :]
        kk = jnp.concatenate([kv0[:, :64], kv1[:, :64]], axis=1)
        kf[here, :] = kk
        vf[here, :] = jnp.concatenate([kv0[:, 64:], kv1[:, 64:]], axis=1)
        allowed = (
            i * 256 + lax.broadcasted_iota(jnp.int32, (rows, 256), 1)
            <= s * rows + lax.broadcasted_iota(jnp.int32, (rows, 256), 0)
        )
        for p in range(nq):
            r = slice(rows * p, rows * p + rows)
            sc = jnp.where(allowed, mm_nt(q_st[r, :], kk) * scale, NEG_FILL)
            s_buf[i, r, :] = sc
            m_buf[r, :] = jnp.maximum(m_buf[r, :], jnp.maximum(sc[:, :128], sc[:, 128:]))
        return carry

    lax.fori_loop(0, chunk + 1, scores, 0)
    m_buf[...] = jnp.broadcast_to(jnp.max(m_buf[...], axis=1, keepdims=True), (nq * rows, 128))

    def weights(i, carry):
        here = pl.ds(pl.multiple_of(i * 256, 256), 256)
        vv = vf[here, :]
        for p in range(nq):
            r = slice(rows * p, rows * p + rows)
            m = m_buf[r, :]
            e = jnp.exp(s_buf[i, r, :] - jnp.concatenate([m, m], axis=1))
            s_buf[i, r, :] = e
            l_buf[r, :] += e[:, :128] + e[:, 128:]
            acc[r, :] += mm(e.astype(BF16), vv)
        return carry

    lax.fori_loop(0, chunk + 1, weights, 0)
    total = jnp.sum(l_buf[...], axis=1, keepdims=True)
    inv = jnp.broadcast_to(1.0 / total, (nq * rows, 128))
    l_buf[...] = inv
    acc[...] = acc[...] * inv
    for p in range(nq):
        x_v[:, 128 * p:128 * p + 128] = acc[128 * p:128 * p + 128, :]

    xw = (x_v[...] * w2x[...]).astype(BF16)
    fs_send[...] = mm_tn(xw, write_v[...]).astype(BF16)
    fs_copy = all_to_all(fs_send, fs_recv, fs_ss, fs_rs)

    m_sum = jnp.zeros((rows, rows), F32)
    col_r = jnp.zeros((nheads, rows), F32)
    row_r = jnp.zeros((nheads, rows), F32)
    ones8 = jnp.ones((8, 128), F32)
    for p in range(nheads // 2):
        lanes = slice(128 * p, 128 * p + 128)
        xp = x_v[:, lanes]
        g = mm_nt(gym_b[p], xp.astype(BF16))
        mp = dtl_b[p] * g
        m_sum = m_sum + mp[:rows] + mp[rows:]
        r0 = mp[:rows] * cb
        r1 = mp[rows:] * cb
        rs = mm_nt(ones8, jnp.concatenate([r0, r1], axis=0), HIGH)
        col_r = jnp.where(head_i == 2 * p, jnp.sum(r0, axis=0, keepdims=True), col_r)
        col_r = jnp.where(head_i == 2 * p + 1, jnp.sum(r1, axis=0, keepdims=True), col_r)
        row_r = jnp.where(head_i == 2 * p, rs[0:1, :rows], row_r)
        row_r = jnp.where(head_i == 2 * p + 1, rs[0:1, rows:], row_r)

    wait_from(lambda j: rcopy(seq_block(ex_recv, j, 64), seq_block(ex_recv, j, 64), ex_ss.at[0], ex_rs.at[j], seq=j))
    exit_g = ex_recv[...]
    dx_exit = mm_nt(write_v[...], exit_g) * w2x[...]
    r_s = mm_nt(eb64, x_v[...] * dx_exit, HIGH)
    gyx = mm_nt(eb64, x_v[...] * gy[...], HIGH)
    dx[...] = dx[...] + dx_exit
    grad_w = mm_tn(m_sum.astype(BF16), read_v[...]) + mm(xw, exit_g)
    ps_send[:rows, :] = grad_w.astype(BF16)

    wait_from(lambda j: rcopy(fs_recv.at[j], fs_recv.at[j], fs_ss.at[0], fs_rs.at[j], seq=j))
    state = jnp.zeros((64, 128), F32)
    for i in range(nseq):
        fs_out[i] = state.astype(BF16)
        send_back(fs_out, fi_recv, fi_ss, fi_rs, i)
        state = fs_recv[i].astype(F32) + jnp.exp(-cl_all[i, pl.ds(s, 1), :]) * state

    for p in range(nq):
        r = slice(rows * p, rows * p + rows)
        ga = dx[:, 128 * p:128 * p + 128]
        gl_st[r, :] = ga.astype(BF16)
        delta_b[r, :] = jnp.broadcast_to(
            jnp.sum(ga * x_v[:, 128 * p:128 * p + 128], axis=1, keepdims=True), (rows, 128)
        )
    acc[...] = jnp.zeros((nq * rows, 128), F32)

    def kg_copy(p, j):
        return rcopy(
            kg_send.at[p, pl.ds(pl.multiple_of(j * rows, rows), rows)], kg_recv.at[par, s],
            kg_ss.at[p, j], kg_rs.at[par, s], seq=j, tp=base + p,
        )

    def kg_mine(p, j):
        return jnp.logical_and(j == s, p == par)

    def backward(i, carry):
        here = pl.ds(pl.multiple_of(i * 256, 256), 256)
        kk = kf[here, :]
        vv = vf[here, :]
        gk = jnp.zeros((256, 128), F32)
        gv = jnp.zeros((256, 128), F32)
        for p in range(nq):
            r = slice(rows * p, rows * p + rows)
            iv = l_buf[r, :]
            de = delta_b[r, :]
            pr = s_buf[i, r, :] * jnp.concatenate([iv, iv], axis=1)
            gl = gl_st[r, :]
            ds = (pr * (mm_nt(gl, vv) - jnp.concatenate([de, de], axis=1))).astype(BF16)
            acc[r, :] += mm(ds, kk)
            gv = gv + mm_tn(pr.astype(BF16), gl)
            gk = gk + mm_tn(ds, q_st[r, :])
        gk = gk * scale
        kg_send[0, here, :] = jnp.concatenate([gk[:, :64], gv[:, :64]], axis=1).astype(BF16)
        kg_send[1, here, :] = jnp.concatenate([gk[:, 64:], gv[:, 64:]], axis=1).astype(BF16)
        for c in range(2):
            j = 2 * i + c
            for p in range(2):
                @pl.when(jnp.logical_and(j <= s, jnp.logical_not(kg_mine(p, j))))
                def _(p=p, j=j):
                    kg_copy(p, j).start()
        return carry

    lax.fori_loop(0, chunk + 1, backward, 0)
    kg_recv[par, s] = kg_send[par, own_rows, :]
    for p in range(nq):
        gq_o[:, 128 * p:128 * p + 128] = acc[128 * p:128 * p + 128, :] * scale
    outs = []

    def put(src, dst):
        copy = pltpu.make_async_copy(src, dst, out_sem.at[len(outs)])
        copy.start()
        outs.append(copy)

    put(gq_o, gq_hbm.at[0])

    wait_from(lambda j: rcopy(seq_block(fi_recv, j, 64), seq_block(fi_recv, j, 64), fi_ss.at[0], fi_rs.at[j], seq=j))
    entry = fi_recv[...]
    gye = (gy[...] * ecx[...]).astype(BF16)
    grad_r = mm(m_sum.astype(BF16), write_v[...]) + mm(gye, entry)
    ps_send[rows:, :] = grad_r.astype(BF16)
    part = 2 * rows // ntp

    def p1_copy(d):
        to = lax.rem(z + d, ntp)
        return rcopy(seq_block(ps_send, to, part), ps_recv.at[z], p1_ss.at[d], p1_rs.at[z], tp=to)

    for d in range(1, ntp):
        p1_copy(d).start()
    own_part = pl.ds(pl.multiple_of(z * part, part), part)
    ps_recv[z] = ps_send[own_part, :]

    y_ent = mm_nt(read_v[...], entry) * ecx[...]
    q_t = mm_nt(eb64, gy[...] * y_ent, HIGH)
    for p in range(nheads // 2):
        lanes = slice(128 * p, 128 * p + 128)
        xp = x_v[:, lanes]
        xm = jnp.concatenate([jnp.where(lane_lo, xp, 0.0), jnp.where(lane_lo, 0.0, xp)], axis=0).astype(BF16)
        y = mm(w_b[p], xm) + y_ent[:, lanes] + skip_row[:, lanes] * xp
        gg_o[:, lanes] = dsc[:, lanes] * y
    put(gg_o, gg_hbm.at[0])

    es_prod = exit_g.astype(F32) * entry.astype(F32)
    c_h = jnp.sum(mm(eb64, es_prod, HIGH), axis=1, keepdims=True) * jnp.exp(-cum_last)
    tail = jnp.where(row_i >= col_i, 1.0, 0.0).astype(F32)
    before = jnp.where(row_i < col_i, 1.0, 0.0).astype(F32)
    drate = mm(col_r - row_r - q_t, tail, HIGH) - mm(r_s, before, HIGH) - c_h
    ddt = (col_r + r_s) / dt + drate * ea
    draw = ddt * sig_z
    gdt_o[...] = draw
    put(gdt_o, gdt_hbm.at[0])

    lane8 = lax.broadcasted_iota(jnp.int32, (nheads, 128), 1)
    pp_all[s] = jnp.where(
        lane8 == 0, jnp.sum(drate * rate, axis=1, keepdims=True),
        jnp.where(
            lane8 == 1, jnp.sum(gyx, axis=1, keepdims=True),
            jnp.where(lane8 == 2, jnp.sum(draw, axis=1, keepdims=True), 0.0),
        ),
    )

    def pa_copy(d):
        return rcopy(pp_all.at[s], pp_all.at[s], pa_ss.at[d], pa_rs.at[s], seq=lax.rem(s + d, nseq))

    for d in range(1, nseq):
        pa_copy(d).start()

    for d in range(1, ntp):
        j = lax.rem(z + d, ntp)
        rcopy(ps_recv.at[j], ps_recv.at[j], p1_ss.at[0], p1_rs.at[j], tp=j).wait_recv()
    red = ps_recv[0].astype(F32)
    for j in range(1, ntp):
        red = red + ps_recv[j].astype(F32)
    ps_out[own_part, :] = red.astype(BF16)

    def p2_copy(d):
        here = seq_block(ps_out, z, part)
        return rcopy(here, here, p2_ss.at[d], p2_rs.at[z], tp=lax.rem(z + d, ntp))

    for d in range(1, ntp):
        p2_copy(d).start()

    wait_from(lambda j: rcopy(pp_all.at[j], pp_all.at[j], pa_ss.at[0], pa_rs.at[j], seq=j))
    pd = pp_all[0]
    for j in range(1, nseq):
        pd = pd + pp_all[j]
    pd_all[x] = pd

    def pb_copy(d):
        return rcopy(pd_all.at[x], pd_all.at[x], pb_ss.at[d], pb_rs.at[x], dp=lax.rem(x + d, ndp))

    for d in range(1, ndp):
        pb_copy(d).start()

    def kg_add(j, total):
        for p in range(2):
            @pl.when(jnp.logical_not(kg_mine(p, j)))
            def _(p=p):
                rcopy(kg_recv.at[p, j], kg_recv.at[p, j], kg_ss.at[0, 0], kg_rs.at[p, j], tp=other).wait_recv()
        return total + kg_recv[0, j].astype(F32) + kg_recv[1, j].astype(F32)

    kg = lax.fori_loop(s, nseq, kg_add, jnp.zeros((rows, 128), F32))
    gk_o[...] = kg[:, :64]
    gv_o[...] = kg[:, 64:]
    put(gk_o, gk_hbm.at[0])
    put(gv_o, gv_hbm.at[0])

    for d in range(1, ndp):
        j = lax.rem(x + d, ndp)
        rcopy(pd_all.at[j], pd_all.at[j], pb_ss.at[0], pb_rs.at[j], dp=j).wait_recv()
    pd = pd_all[0]
    for j in range(1, ndp):
        pd = pd + pd_all[j]
    pf[...] = pd
    to_smem = pltpu.make_async_copy(pf, pp_smem, sm_sem)
    to_smem.start()

    for d in range(1, ntp):
        j = lax.rem(z + d, ntp)
        there = seq_block(ps_out, j, part)
        rcopy(there, there, p2_ss.at[0], p2_rs.at[j], tp=j).wait_recv()
    gw_o[...] = ps_out[:rows, :].astype(F32)
    gr_o[...] = ps_out[rows:, :].astype(F32)
    put(gw_o, gw_hbm.at[0])
    put(gr_o, gr_hbm.at[0])

    to_smem.wait()
    for h in range(nheads):
        galog_s[h] = pp_smem[h, 0]
        gskip_s[h] = pp_smem[h, 1]
        gbias_s[h] = pp_smem[h, 2]

    kv_copy(0, 0, s, other).wait_send()
    for d in range(1, nseq):
        @pl.when(s + d < nseq)
        def _(d=d):
            kv_copy(d, 0, s + d, base).wait_send()
            kv_copy(d, 1, s + d, base + 1).wait_send()
        cl_copy(d, lax.rem(s + d, nseq)).wait_send()
        es_copy(d).wait_send()
        fs_copy(d).wait_send()
        pa_copy(d).wait_send()
    for i in range(nseq):
        @pl.when(s != i)
        def _(i=i):
            back_copy(es_out, ex_recv, ex_ss, ex_rs, i).wait_send()
            back_copy(fs_out, fi_recv, fi_ss, fi_rs, i).wait_send()
        for p in range(2):
            @pl.when(jnp.logical_and(i <= s, jnp.logical_not(kg_mine(p, i))))
            def _(p=p, i=i):
                kg_copy(p, i).wait_send()
    for d in range(1, ntp):
        p1_copy(d).wait_send()
        p2_copy(d).wait_send()
    for d in range(1, ndp):
        pb_copy(d).wait_send()
    for copy in outs:
        copy.wait()


def body(
    dims, query_rows, key_rows, value_rows, gate_rows, write_vec, read_vec, dt_raw, a_log, skip_gain, dt_bias, out_grad
):
    nseq, ntp, ndp, nheads, nq = dims
    rows = 128
    wide = nheads * 64
    dma = pltpu.SemaphoreType.DMA

    def vm(shape, kind=F32):
        return pltpu.VMEM(shape, kind)

    any_spec = pl.BlockSpec(memory_space=pl.ANY)
    smem_spec = pl.BlockSpec(memory_space=pltpu.SMEM)
    outs = (
        (1, rows, wide), (1, rows, 64), (1, rows, 64), (1, rows, wide), (1, rows, 128), (1, rows, 128),
        (1, nheads, rows), (nheads,), (nheads,), (nheads,),
    )
    tall = nq * rows
    scratch = [
        vm((rows, wide), BF16), vm((rows, 64), BF16), vm((rows, 64), BF16), vm((rows, wide), BF16),
        vm((rows, 128), BF16), vm((rows, 128), BF16), vm((nheads, rows)), vm((rows, wide), BF16),
        vm((2, nseq * rows, 128), BF16), vm((nseq * rows, 128), BF16), vm((nseq * rows, 128), BF16),
        vm((tall, 128), BF16), vm((nseq // 2, tall, 256)), vm((tall, 128)), vm((tall, 128)), vm((tall, 128)),
        vm((tall, 128), BF16), vm((tall, 128)),
        vm((rows, wide)), vm((rows, wide)), vm((rows, wide)), vm((rows, wide)), vm((rows, wide)), vm((rows, wide)),
        vm((nheads // 2, 2 * rows, rows)), vm((nheads // 2, rows, 2 * rows), BF16),
        vm((nheads // 2, 2 * rows, 128), BF16),
        vm((nseq, nheads, 128)),
        vm((wide, 128), BF16), vm((nseq, 64, 128), BF16), vm((nseq, 64, 128), BF16), vm((wide, 128), BF16),
        vm((wide, 128), BF16), vm((nseq, 64, 128), BF16), vm((nseq, 64, 128), BF16), vm((wide, 128), BF16),
        vm((2, nseq * rows, 128), BF16), vm((2, nseq, rows, 128), BF16),
        vm((2 * rows, 128), BF16), vm((ntp, 2 * rows // ntp, 128), BF16), vm((2 * rows, 128), BF16),
        vm((nseq, nheads, 128)), vm((ndp, nheads, 128)), vm((nheads, 128)), pltpu.SMEM((nheads, 128), F32),
        vm((rows, wide)), vm((rows, 64)), vm((rows, 64)), vm((rows, wide)), vm((rows, 128)), vm((rows, 128)),
        vm((nheads, rows)),
        dma((8,)), dma((7,)), dma((nseq, 2)), dma((2, nseq)), dma((nseq,)), dma((nseq,)),
        dma((nseq,)), dma((nseq,)), dma((nseq,)), dma((nseq,)),
        dma((nseq,)), dma((nseq,)), dma((nseq,)), dma((nseq,)),
        dma((2, nseq)), dma((2, nseq)), dma((ntp,)), dma((ntp,)), dma((ntp,)), dma((ntp,)),
        dma((nseq,)), dma((nseq,)), dma((ndp,)), dma((ndp,)), dma(()),
    ]
    return pl.pallas_call(
        functools.partial(kernel, dims),
        out_shape=tuple(jax.ShapeDtypeStruct(o, F32) for o in outs),
        in_specs=[any_spec] * 8 + [smem_spec] * 3,
        out_specs=tuple([any_spec] * 7 + [smem_spec] * 3),
        scratch_shapes=scratch,
        compiler_params=pltpu.CompilerParams(
            collective_id=0, has_side_effects=True, vmem_limit_bytes=48 * 1024 * 1024
        ),
    )(query_rows, key_rows, value_rows, gate_rows, write_vec, read_vec, dt_raw, out_grad, a_log, skip_gain, dt_bias)


def solution(mesh):
    dims = (mesh.shape["seq"], mesh.shape["tp"], mesh.shape["dp"], 8, 4)
    wide = P("dp", "seq", "tp")
    shared = P("dp", "seq", None)
    steps = P("dp", "tp", "seq")
    head = P("tp")
    return jax.shard_map(
        functools.partial(body, dims),
        mesh=mesh,
        in_specs=(wide, wide, wide, wide, shared, shared, steps, head, head, head, wide),
        out_specs=(wide, wide, wide, wide, shared, shared, steps, head, head, head),
        check_vma=False,
    )
```

time: 370 us -> 68 us (0.18)
  waiting for transfers between devices: 167 us -> 0 us
  blocking collectives: 124 us -> 0 us
  Pallas kernels: 0 us -> 55.8 us
  other arithmetic: 22.2 us -> 0 us
  between operations: 14.9 us -> 0.75 us
  matrix products: 12.7 us -> 0 us
  starting transfers between devices: 11 us -> 0 us
    unnamed x7 -> x0, waiting for transfers between devices: 79.9 us -> none
    psum x1 -> x0, blocking collectives: 64.1 us -> none  [body(): lax.psum((main_alog + entry_alog, main_skip, main_bias + entry_bias), ('s...]
    pallas_call x0 -> x1, Pallas kernels: none -> 55.8 us  [body(): pl.pallas_call(functools.partial(kernel, dims), out_shape=tuple((jax.Shap...]
    psum x1 -> x0, waiting for transfers between devices: 54.2 us -> none  [body(): lax.psum(main_write.astype(jnp.bfloat16), 'tp').astype(jnp.float32)]
    all_gather x2 -> x0, blocking collectives: 31.9 us -> none  [the longest x1 19.1 us: body(): lax.all_gather(local_keys, 'seq', axis=0, tiled=True)]
    all_gather x2 -> x0, waiting for transfers between devices: 31.6 us -> none  [the longest x1 17.1 us: prefix(): everything = jax.tree.map(lambda part: lax.all_gather(part, axis), array)]
    unnamed x2 -> x0, blocking collectives: 28.4 us -> none
    dot_general x21 -> x0, matrix products: 12.7 us -> none  [the longest x3 4.12 us: advance(): output = jnp.einsum('hts,shp->thp', weight, inner_now, precision=HIGH)]
  transfers between devices with their start and end apart: 9 -> 0, of which waited for: 6 -> 0; matrix products, arithmetic and copies ran while one was open for 7% -> 0% of each run, Pallas kernels for 0% -> 0%
where the time goes in v1:
time: 68 us; the launch traced here: 67 us
  Pallas kernels  55.8 us (82%)
  local copies, waits for them, and re-layouts  10.5 us (15%)
  between operations  0.75 us (1%)
    pallas_call x1, Pallas kernels, body(): pl.pallas_call(functools.partial(kernel, dims), out_shape=tuple((jax.Shap...  55.8 us
    unnamed x30, local copies, waits for them, and re-layouts  9.06 us
    pallas_call x2, local copies, waits for them, and re-layouts, body(): pl.pallas_call(functools.partial(kernel, dims), out_shape=tuple((jax.Shap...  1.4 us

profile of v1, /device:TPU:1, one launch (start us, length us, event | category | flops | bytes accessed | tf_op | source)
XLA Modules:
  0.0 67.0 jit_solution(15937573176328668217)
XLA Ops:
  0.6 0.0 copy-start.9
  0.7 0.8 %copy.21.k_hbm = bf16[1,128,64]{2,1,0:T(8,128)(2,1)S(1)} copy(bf16[1,128,64]{1,2,0:T(8,128)(2,1)} %param.12) | data formatting | bytes 32768 | tf_op args[1]
  1.5 0.0 copy-start.3
  1.5 0.0 copy-start.5
  1.5 0.0 copy-start.6
  1.5 0.0 copy-start.7
  1.6 0.0 copy-start.8
  1.6 0.1 copy.22.v_hbm
  1.7 0.6 copy-done.3
  2.3 0.0 copy-start
  2.3 0.9 %copy-done = bf16[1,128,512]{2,1,0:T(8,128)(2,1)S(1)} copy-done((bf16[1,128,512]{2,1,0:T(8,128)(2,1)S(1)}, bf16[1,128,512]{2,1,0:T(8,128)(2,1)}, u32[]{:S(2)}) %copy-start) | copy-done | bytes 131096
  3.2 0.9 %copy-done.1 = bf16[1,128,512]{2,1,0:T(8,128)(2,1)S(1)} copy-done((bf16[1,128,512]{2,1,0:T(8,128)(2,1)S(1)}, bf16[1,128,512]{2,1,0:T(8,128)(2,1)}, u32[]{:S(2)}) %copy-start.1) | copy-done | bytes 131096
  4.1 0.9 %copy-done.2 = bf16[1,128,512]{2,1,0:T(8,128)(2,1)S(1)} copy-done((bf16[1,128,512]{2,1,0:T(8,128)(2,1)S(1)}, bf16[1,128,512]{2,1,0:T(8,128)(2,1)}, u32[]{:S(2)}) %copy-start.2) | copy-done | bytes 131096
  5.0 55.8 %shard_map.186 = (f32[1,128,512]{2,1,0:T(8,128)S(1)}, f32[1,128,64]{2,1,0:T(8,128)S(1)}, f32[1,128,64]{2,1,0:T(8,128)S(1)}, f32[1,128,512]{2,1,0:T(8,128)S(1)}, ...) custom-call(bf16[1,128,512]{2,1,0:T(8,128)(2,1)S(1)} %copy-done, ...), custom_call_target="tpu_custom_call" | custom-call | tf_op jit(solution)/shard_map/pallas_call | solution.py:556
  60.8 0.7 %copy.23 = f32[1,128,64]{1,2,0:T(8,128)} copy(f32[1,128,64]{2,1,0:T(8,128)S(1)} %get-tuple-element.11) | data formatting | bytes 65536 | tf_op jit(solution)/shard_map/pallas_call | solution.py:556
  61.5 0.7 %copy.24 = f32[1,128,64]{1,2,0:T(8,128)} copy(f32[1,128,64]{2,1,0:T(8,128)S(1)} %get-tuple-element.12) | data formatting | bytes 65536 | tf_op jit(solution)/shard_map/pallas_call | solution.py:556
  62.2 0.7 %copy.33 = f32[1,128,512]{2,1,0:T(8,128)} copy(f32[1,128,512]{2,1,0:T(8,128)S(1)} %get-tuple-element.30) | data formatting | bytes 524288
  62.9 0.7 %copy.34 = f32[1,128,512]{2,1,0:T(8,128)} copy(f32[1,128,512]{2,1,0:T(8,128)S(1)} %get-tuple-element.33) | data formatting | bytes 524288
  63.6 0.6 copy.35
  64.2 0.6 copy.36
  64.9 0.6 copy.37
  65.5 0.5 copy.38
  66.0 0.5 copy.39
  66.5 0.5 copy.40
  (9 shorter events, 0.0 us)
Async XLA Ops:
  0.6 0.9 %copy-start.9 = (bf16[1,128,64]{1,2,0:T(8,128)(2,1)S(1)}, bf16[1,128,64]{1,2,0:T(8,128)(2,1)}, u32[]{:S(2)}) copy-start(bf16[1,128,64]{1,2,0:T(8,128)(2,1)} %param.13) | copy-start | bytes 49156
  0.7 1.0 %copy-start.4 = (bf16[1,128,128]{2,1,0:T(8,128)(2,1)S(1)}, bf16[1,128,128]{2,1,0:T(8,128)(2,1)}, u32[]{:S(2)}) copy-start(bf16[1,128,128]{2,1,0:T(8,128)(2,1)} %read_hbm.1) | copy-start | bytes 98308
  1.5 0.8 %copy-start.3 = (bf16[1,128,128]{2,1,0:T(8,128)(2,1)S(1)}, bf16[1,128,128]{2,1,0:T(8,128)(2,1)}, u32[]{:S(2)}) copy-start(bf16[1,128,128]{2,1,0:T(8,128)(2,1)} %write_hbm.1) | copy-start | bytes 98308
  1.5 0.8 %copy-start.5 = (f32[1,8,128]{2,1,0:T(8,128)S(1)}, f32[1,8,128]{2,1,0:T(8,128)}, u32[]{:S(2)}) copy-start(f32[1,8,128]{2,1,0:T(8,128)} %dt_hbm.1) | copy-start | bytes 12292
  1.5 0.7 %copy-start.6 = (f32[8]{0:T(128)S(1)}, f32[8]{0:T(128)}, u32[]{:S(2)}) copy-start(f32[8]{0:T(128)} %alog_s.1) | copy-start | bytes 100
  1.5 0.7 %copy-start.7 = (f32[8]{0:T(128)S(1)}, f32[8]{0:T(128)}, u32[]{:S(2)}) copy-start(f32[8]{0:T(128)} %skip_s.1) | copy-start | bytes 100
  1.6 0.7 %copy-start.8 = (f32[8]{0:T(128)S(1)}, f32[8]{0:T(128)}, u32[]{:S(2)}) copy-start(f32[8]{0:T(128)} %bias_s.1) | copy-start | bytes 100
  2.3 0.9 %copy-start = (bf16[1,128,512]{2,1,0:T(8,128)(2,1)S(1)}, bf16[1,128,512]{2,1,0:T(8,128)(2,1)}, u32[]{:S(2)}) copy-start(bf16[1,128,512]{2,1,0:T(8,128)(2,1)} %q_hbm.1) | copy-start | bytes 393220
  3.2 0.9 %copy-start.1 = (bf16[1,128,512]{2,1,0:T(8,128)(2,1)S(1)}, bf16[1,128,512]{2,1,0:T(8,128)(2,1)}, u32[]{:S(2)}) copy-start(bf16[1,128,512]{2,1,0:T(8,128)(2,1)} %gate_hbm.1) | copy-start | bytes 393220
  4.1 0.9 %copy-start.2 = (bf16[1,128,512]{2,1,0:T(8,128)(2,1)S(1)}, bf16[1,128,512]{2,1,0:T(8,128)(2,1)}, u32[]{:S(2)}) copy-start(bf16[1,128,512]{2,1,0:T(8,128)(2,1)} %cot_hbm.1) | copy-start | bytes 393220

commit v2 on v1

--- a/solution.py
+++ b/solution.py
@@ -12,6 +12,7 @@
 F32 = jnp.float32
 BF16 = jnp.bfloat16
 NEG_FILL = -1e30
+VMEM = 60 * 1024 * 1024
 
 
 def mm(a, b, precision=None):
@@ -30,15 +31,15 @@
     dims,
     q_hbm, k_hbm, v_hbm, gate_hbm, write_hbm, read_hbm, dt_hbm, cot_hbm,
     alog_s, skip_s, bias_s,
-    gq_hbm, gk_hbm, gv_hbm, gg_hbm, gw_hbm, gr_hbm, gdt_hbm, galog_s, gskip_s, gbias_s,
+    gq_hbm, gk_hbm, gv_hbm, gg_hbm, gw_hbm, gr_hbm, gdt_hbm, pf_hbm,
     q_v, k_v, v_v, gate_v, write_v, read_v, dt_v, cot_v,
-    kv_buf, kf, vf, q_st, s_buf, m_buf, l_buf, acc, gl_st, delta_b,
+    kv_buf, kf, vf, q_st, q_t, s_buf, m_buf, l_buf, acc, gl_st, gl_t, delta_b,
     gy, dsc, ecx, w2x, dx, x_v, dtl_b, w_b, gym_b,
     cl_all, es_send, es_recv, es_out, ex_recv, fs_send, fs_recv, fs_out, fi_recv,
-    kg_send, kg_recv, ps_send, ps_recv, ps_out, pp_all, pd_all, pf, pp_smem,
-    gq_o, gk_o, gv_o, gg_o, gw_o, gr_o, gdt_o,
+    kg_send, kg_recv, ps_send, ps_recv, ps_out, pp_all, pd_all,
+    gq_o, gk_o, gv_o, gg_o, gw_o, gr_o, gdt_o, pf,
     in_sem, out_sem, kv_ss, kv_rs, cl_ss, cl_rs, es_ss, es_rs, ex_ss, ex_rs, fs_ss, fs_rs, fi_ss, fi_rs,
-    kg_ss, kg_rs, p1_ss, p1_rs, p2_ss, p2_rs, pa_ss, pa_rs, pb_ss, pb_rs, sm_sem,
+    kg_ss, kg_rs, p1_ss, p1_rs, p2_ss, p2_rs, pa_ss, pa_rs, pb_ss, pb_rs,
 ):
     nseq, ntp, ndp, nheads, nq = dims
     rows = 128
@@ -59,6 +60,13 @@
     def seq_block(ref, i, n):
         return ref.at[pl.ds(pl.multiple_of(i * n, n), n)]
 
+    outs = []
+
+    def put(src, dst):
+        copy = pltpu.make_async_copy(src, dst, out_sem.at[len(outs)])
+        copy.start()
+        outs.append(copy)
+
     loads = []
     for at, (src, dst) in enumerate((
         (k_hbm.at[0], k_v), (v_hbm.at[0], v_v), (dt_hbm.at[0], dt_v), (gate_hbm.at[0], gate_v),
@@ -80,19 +88,17 @@
 
     loads[0].wait()
     loads[1].wait()
-    own_rows = pl.ds(pl.multiple_of(s * rows, rows), rows)
-    kv_buf[par, own_rows, :] = jnp.concatenate([k_v[...], v_v[...]], axis=1)
+    kv_buf[par, s] = jnp.concatenate([k_v[...], v_v[...]], axis=0)
 
     @pl.when(lax.rem(s, 2) == 0)
     def _():
-        blank = pl.ds(pl.multiple_of((s + 1) * rows, rows), rows)
-        kv_buf[0, blank, :] = jnp.zeros((rows, 128), BF16)
-        kv_buf[1, blank, :] = jnp.zeros((rows, 128), BF16)
+        kv_buf[0, s + 1] = jnp.zeros((rows, 128), BF16)
+        kv_buf[1, s + 1] = jnp.zeros((rows, 128), BF16)
 
     pl.semaphore_wait(barrier, 2 * (nseq - 1) + (ntp - 1) + (ndp - 1))
 
     def kv_copy(d, p, to_seq, to_tp):
-        here = kv_buf.at[par, own_rows]
+        here = kv_buf.at[par, s]
         return rcopy(here, here, kv_ss.at[d, p], kv_rs.at[par, s], seq=to_seq, tp=to_tp)
 
     kv_copy(0, 0, s, other).start()
@@ -220,31 +226,31 @@
     loads[7].wait()
     for p in range(nq):
         q_st[128 * p:128 * p + 128, :] = q_v[:, 128 * p:128 * p + 128]
+        q_t[:, 128 * p:128 * p + 128] = q_v[:, 128 * p:128 * p + 128].T
     m_buf[...] = jnp.full((nq * rows, 128), NEG_FILL, F32)
     l_buf[...] = jnp.zeros((nq * rows, 128), F32)
     acc[...] = jnp.zeros((nq * rows, 128), F32)
 
     def scores(i, carry):
-        here = pl.ds(pl.multiple_of(i * 256, 256), 256)
         for c in range(2):
             j = 2 * i + c
             for p in range(2):
                 @pl.when(jnp.logical_and(j <= s, jnp.logical_or(j != s, p != par)))
                 def _(p=p, j=j):
-                    slot = kv_buf.at[p, pl.ds(pl.multiple_of(j * rows, rows), rows)]
+                    slot = kv_buf.at[p, j]
                     rcopy(slot, slot, kv_ss.at[0, 0], kv_rs.at[p, j], tp=other).wait_recv()
-        kv0 = kv_buf[0, here, :]
-        kv1 = kv_buf[1, here, :]
-        kk = jnp.concatenate([kv0[:, :64], kv1[:, :64]], axis=1)
-        kf[here, :] = kk
-        vf[here, :] = jnp.concatenate([kv0[:, 64:], kv1[:, 64:]], axis=1)
+        lo = jnp.concatenate([kv_buf[0, 2 * i], kv_buf[0, 2 * i + 1]], axis=1)
+        hi = jnp.concatenate([kv_buf[1, 2 * i], kv_buf[1, 2 * i + 1]], axis=1)
+        kk = jnp.concatenate([lo[:64], hi[:64]], axis=0)
+        kf[i] = kk
+        vf[i] = jnp.concatenate([lo[64:], hi[64:]], axis=0)
         allowed = (
             i * 256 + lax.broadcasted_iota(jnp.int32, (rows, 256), 1)
             <= s * rows + lax.broadcasted_iota(jnp.int32, (rows, 256), 0)
         )
         for p in range(nq):
             r = slice(rows * p, rows * p + rows)
-            sc = jnp.where(allowed, mm_nt(q_st[r, :], kk) * scale, NEG_FILL)
+            sc = jnp.where(allowed, mm(q_st[r, :], kk) * scale, NEG_FILL)
             s_buf[i, r, :] = sc
             m_buf[r, :] = jnp.maximum(m_buf[r, :], jnp.maximum(sc[:, :128], sc[:, 128:]))
         return carry
@@ -253,15 +259,14 @@
     m_buf[...] = jnp.broadcast_to(jnp.max(m_buf[...], axis=1, keepdims=True), (nq * rows, 128))
 
     def weights(i, carry):
-        here = pl.ds(pl.multiple_of(i * 256, 256), 256)
-        vv = vf[here, :]
+        vv = vf[i]
         for p in range(nq):
             r = slice(rows * p, rows * p + rows)
             m = m_buf[r, :]
             e = jnp.exp(s_buf[i, r, :] - jnp.concatenate([m, m], axis=1))
             s_buf[i, r, :] = e
             l_buf[r, :] += e[:, :128] + e[:, 128:]
-            acc[r, :] += mm(e.astype(BF16), vv)
+            acc[r, :] += mm_nt(e.astype(BF16), vv)
         return carry
 
     lax.fori_loop(0, chunk + 1, weights, 0)
@@ -314,6 +319,7 @@
         r = slice(rows * p, rows * p + rows)
         ga = dx[:, 128 * p:128 * p + 128]
         gl_st[r, :] = ga.astype(BF16)
+        gl_t[:, r] = ga.astype(BF16).T
         delta_b[r, :] = jnp.broadcast_to(
             jnp.sum(ga * x_v[:, 128 * p:128 * p + 128], axis=1, keepdims=True), (rows, 128)
         )
@@ -321,7 +327,7 @@
 
     def kg_copy(p, j):
         return rcopy(
-            kg_send.at[p, pl.ds(pl.multiple_of(j * rows, rows), rows)], kg_recv.at[par, s],
+            kg_send.at[p, j], kg_recv.at[par, s],
             kg_ss.at[p, j], kg_rs.at[par, s], seq=j, tp=base + p,
         )
 
@@ -329,24 +335,26 @@
         return jnp.logical_and(j == s, p == par)
 
     def backward(i, carry):
-        here = pl.ds(pl.multiple_of(i * 256, 256), 256)
-        kk = kf[here, :]
-        vv = vf[here, :]
-        gk = jnp.zeros((256, 128), F32)
-        gv = jnp.zeros((256, 128), F32)
+        kk = kf[i]
+        vv = vf[i]
+        gk = jnp.zeros((128, 256), F32)
+        gv = jnp.zeros((128, 256), F32)
         for p in range(nq):
             r = slice(rows * p, rows * p + rows)
             iv = l_buf[r, :]
             de = delta_b[r, :]
             pr = s_buf[i, r, :] * jnp.concatenate([iv, iv], axis=1)
-            gl = gl_st[r, :]
-            ds = (pr * (mm_nt(gl, vv) - jnp.concatenate([de, de], axis=1))).astype(BF16)
-            acc[r, :] += mm(ds, kk)
-            gv = gv + mm_tn(pr.astype(BF16), gl)
-            gk = gk + mm_tn(ds, q_st[r, :])
-        gk = gk * scale
-        kg_send[0, here, :] = jnp.concatenate([gk[:, :64], gv[:, :64]], axis=1).astype(BF16)
-        kg_send[1, here, :] = jnp.concatenate([gk[:, 64:], gv[:, 64:]], axis=1).astype(BF16)
+            ds = (pr * (mm(gl_st[r, :], vv) - jnp.concatenate([de, de], axis=1))).astype(BF16)
+            acc[r, :] += mm_nt(ds, kk)
+            gv = gv + mm(gl_t[:, r], pr.astype(BF16))
+            gk = gk + mm(q_t[:, r], ds)
+        gk = (gk * scale).astype(BF16)
+        gv = gv.astype(BF16)
+        for c in range(2):
+            for p in range(2):
+                kg_send[p, 2 * i + c] = jnp.concatenate(
+                    [gk[64 * p:64 * p + 64, 128 * c:128 * c + 128], gv[64 * p:64 * p + 64, 128 * c:128 * c + 128]], axis=0
+                )
         for c in range(2):
             j = 2 * i + c
             for p in range(2):
@@ -356,18 +364,10 @@
         return carry
 
     lax.fori_loop(0, chunk + 1, backward, 0)
-    kg_recv[par, s] = kg_send[par, own_rows, :]
+    kg_recv[par, s] = kg_send[par, s]
     for p in range(nq):
         gq_o[:, 128 * p:128 * p + 128] = acc[128 * p:128 * p + 128, :] * scale
-    outs = []
-
-    def put(src, dst):
-        copy = pltpu.make_async_copy(src, dst, out_sem.at[len(outs)])
-        copy.start()
-        outs.append(copy)
-
     put(gq_o, gq_hbm.at[0])
-
     wait_from(lambda j: rcopy(seq_block(fi_recv, j, 64), seq_block(fi_recv, j, 64), fi_ss.at[0], fi_rs.at[j], seq=j))
     entry = fi_recv[...]
     gye = (gy[...] * ecx[...]).astype(BF16)
@@ -385,7 +385,7 @@
     ps_recv[z] = ps_send[own_part, :]
 
     y_ent = mm_nt(read_v[...], entry) * ecx[...]
-    q_t = mm_nt(eb64, gy[...] * y_ent, HIGH)
+    q_sum = mm_nt(eb64, gy[...] * y_ent, HIGH)
     for p in range(nheads // 2):
         lanes = slice(128 * p, 128 * p + 128)
         xp = x_v[:, lanes]
@@ -398,7 +398,7 @@
     c_h = jnp.sum(mm(eb64, es_prod, HIGH), axis=1, keepdims=True) * jnp.exp(-cum_last)
     tail = jnp.where(row_i >= col_i, 1.0, 0.0).astype(F32)
     before = jnp.where(row_i < col_i, 1.0, 0.0).astype(F32)
-    drate = mm(col_r - row_r - q_t, tail, HIGH) - mm(r_s, before, HIGH) - c_h
+    drate = mm(col_r - row_r - q_sum, tail, HIGH) - mm(r_s, before, HIGH) - c_h
     ddt = (col_r + r_s) / dt + drate * ea
     draw = ddt * sig_z
     gdt_o[...] = draw
@@ -454,8 +454,8 @@
         return total + kg_recv[0, j].astype(F32) + kg_recv[1, j].astype(F32)
 
     kg = lax.fori_loop(s, nseq, kg_add, jnp.zeros((rows, 128), F32))
-    gk_o[...] = kg[:, :64]
-    gv_o[...] = kg[:, 64:]
+    gk_o[...] = kg[:64]
+    gv_o[...] = kg[64:]
     put(gk_o, gk_hbm.at[0])
     put(gv_o, gv_hbm.at[0])
 
@@ -466,8 +466,7 @@
     for j in range(1, ndp):
         pd = pd + pd_all[j]
     pf[...] = pd
-    to_smem = pltpu.make_async_copy(pf, pp_smem, sm_sem)
-    to_smem.start()
+    put(pf, pf_hbm)
 
     for d in range(1, ntp):
         j = lax.rem(z + d, ntp)
@@ -477,12 +476,6 @@
     gr_o[...] = ps_out[rows:, :].astype(F32)
     put(gw_o, gw_hbm.at[0])
     put(gr_o, gr_hbm.at[0])
-
-    to_smem.wait()
-    for h in range(nheads):
-        galog_s[h] = pp_smem[h, 0]
-        gskip_s[h] = pp_smem[h, 1]
-        gbias_s[h] = pp_smem[h, 2]
 
     kv_copy(0, 0, s, other).wait_send()
     for d in range(1, nseq):
@@ -526,43 +519,72 @@
     any_spec = pl.BlockSpec(memory_space=pl.ANY)
     smem_spec = pl.BlockSpec(memory_space=pltpu.SMEM)
     outs = (
-        (1, rows, wide), (1, rows, 64), (1, rows, 64), (1, rows, wide), (1, rows, 128), (1, rows, 128),
-        (1, nheads, rows), (nheads,), (nheads,), (nheads,),
+        (1, rows, wide), (1, 64, rows), (1, 64, rows), (1, rows, wide), (1, rows, 128), (1, rows, 128),
+        (1, nheads, rows), (nheads, 128),
     )
     tall = nq * rows
     scratch = [
-        vm((rows, wide), BF16), vm((rows, 64), BF16), vm((rows, 64), BF16), vm((rows, wide), BF16),
+        vm((rows, wide), BF16), vm((64, rows), BF16), vm((64, rows), BF16), vm((rows, wide), BF16),
         vm((rows, 128), BF16), vm((rows, 128), BF16), vm((nheads, rows)), vm((rows, wide), BF16),
-        vm((2, nseq * rows, 128), BF16), vm((nseq * rows, 128), BF16), vm((nseq * rows, 128), BF16),
-        vm((tall, 128), BF16), vm((nseq // 2, tall, 256)), vm((tall, 128)), vm((tall, 128)), vm((tall, 128)),
-        vm((tall, 128), BF16), vm((tall, 128)),
+        vm((2, nseq, 128, rows), BF16), vm((nseq // 2, 128, 2 * rows), BF16), vm((nseq // 2, 128, 2 * rows), BF16),
+        vm((tall, 128), BF16), vm((128, tall), BF16), vm((nseq // 2, tall, 256)), vm((tall, 128)), vm((tall, 128)), vm((tall, 128)),
+        vm((tall, 128), BF16), vm((128, tall), BF16), vm((tall, 128)),
         vm((rows, wide)), vm((rows, wide)), vm((rows, wide)), vm((rows, wide)), vm((rows, wide)), vm((rows, wide)),
         vm((nheads // 2, 2 * rows, rows)), vm((nheads // 2, rows, 2 * rows), BF16),
         vm((nheads // 2, 2 * rows, 128), BF16),
         vm((nseq, nheads, 128)),
         vm((wide, 128), BF16), vm((nseq, 64, 128), BF16), vm((nseq, 64, 128), BF16), vm((wide, 128), BF16),
         vm((wide, 128), BF16), vm((nseq, 64, 128), BF16), vm((nseq, 64, 128), BF16), vm((wide, 128), BF16),
-        vm((2, nseq * rows, 128), BF16), vm((2, nseq, rows, 128), BF16),
+        vm((2, nseq, 128, rows), BF16), vm((2, nseq, 128, rows), BF16),
         vm((2 * rows, 128), BF16), vm((ntp, 2 * rows // ntp, 128), BF16), vm((2 * rows, 128), BF16),
-        vm((nseq, nheads, 128)), vm((ndp, nheads, 128)), vm((nheads, 128)), pltpu.SMEM((nheads, 128), F32),
-        vm((rows, wide)), vm((rows, 64)), vm((rows, 64)), vm((rows, wide)), vm((rows, 128)), vm((rows, 128)),
-        vm((nheads, rows)),
-        dma((8,)), dma((7,)), dma((nseq, 2)), dma((2, nseq)), dma((nseq,)), dma((nseq,)),
+        vm((nseq, nheads, 128)), vm((ndp, nheads, 128)),
+        vm((rows, wide)), vm((64, rows)), vm((64, rows)), vm((rows, wide)), vm((rows, 128)), vm((rows, 128)),
+        vm((nheads, rows)), vm((nheads, 128)),
+        dma((8,)), dma((8,)), dma((nseq, 2)), dma((2, nseq)), dma((nseq,)), dma((nseq,)),
         dma((nseq,)), dma((nseq,)), dma((nseq,)), dma((nseq,)),
         dma((nseq,)), dma((nseq,)), dma((nseq,)), dma((nseq,)),
         dma((2, nseq)), dma((2, nseq)), dma((ntp,)), dma((ntp,)), dma((ntp,)), dma((ntp,)),
-        dma((nseq,)), dma((nseq,)), dma((ndp,)), dma((ndp,)), dma(()),
+        dma((nseq,)), dma((nseq,)), dma((ndp,)), dma((ndp,)),
     ]
-    return pl.pallas_call(
+    results = pl.pallas_call(
         functools.partial(kernel, dims),
         out_shape=tuple(jax.ShapeDtypeStruct(o, F32) for o in outs),
         in_specs=[any_spec] * 8 + [smem_spec] * 3,
-        out_specs=tuple([any_spec] * 7 + [smem_spec] * 3),
+        out_specs=tuple([any_spec] * 8),
         scratch_shapes=scratch,
         compiler_params=pltpu.CompilerParams(
-            collective_id=0, has_side_effects=True, vmem_limit_bytes=48 * 1024 * 1024
+            collective_id=0, has_side_effects=True, vmem_limit_bytes=VMEM
         ),
-    )(query_rows, key_rows, value_rows, gate_rows, write_vec, read_vec, dt_raw, out_grad, a_log, skip_gain, dt_bias)
+    )(
+        query_rows, jnp.swapaxes(key_rows, 1, 2), jnp.swapaxes(value_rows, 1, 2), gate_rows, write_vec, read_vec, dt_raw,
+        out_grad, a_log, skip_gain, dt_bias,
+    )
+    per_head = jax.ShapeDtypeStruct((nheads,), F32)
+    written = pl.pallas_call(
+        functools.partial(write_out, nheads),
+        out_shape=tuple([jax.ShapeDtypeStruct(o, F32) for o in outs[:7]] + [per_head] * 3),
+        in_specs=[any_spec] * 8,
+        out_specs=tuple([any_spec] * 7 + [smem_spec] * 3),
+        scratch_shapes=[dma((8,)), pltpu.SMEM((nheads, 128), F32)],
+        compiler_params=pltpu.CompilerParams(vmem_limit_bytes=VMEM),
+    )(*results)
+    return (
+        written[0], jnp.swapaxes(written[1], 1, 2), jnp.swapaxes(written[2], 1, 2), *written[3:],
+    )
+
+
+def write_out(nheads, *refs):
+    sources, targets, (sems, small) = refs[:8], refs[8:18], refs[18:]
+    copies = [pltpu.make_async_copy(sources[7], small, sems.at[7])]
+    copies += [pltpu.make_async_copy(a, b, sems.at[i]) for i, (a, b) in enumerate(zip(sources[:7], targets[:7]))]
+    for copy in copies:
+        copy.start()
+    copies[0].wait()
+    for h in range(nheads):
+        for i in range(3):
+            targets[7 + i][h] = small[h, i]
+    for copy in copies[1:]:
+        copy.wait()
 
 
 def solution(mesh):

time: 68 us -> 82.3 us (1.21)
  the two profiles are of different devices: /device:TPU:1 before, /device:TPU:8 now
where the time goes in v2:
time: 82.3 us; the launch traced here: 82 us
  Pallas kernels  81.3 us (99%)
    pallas_call x1, Pallas kernels, body(): pl.pallas_call(functools.partial(kernel, dims), out_shape=tuple((jax.Shap...  57.7 us
    pallas_call x1, Pallas kernels, body(): pl.pallas_call(functools.partial(write_out, nheads), out_shape=tuple([jax...  23.7 us

profile of v2, /device:TPU:8, one launch (start us, length us, event | category | flops | bytes accessed | tf_op | source)
XLA Modules:
  0.0 82.0 jit_solution(13352640143006908516)
XLA Ops:
  0.6 57.7 %shard_map.186 = (f32[1,128,512]{2,1,0:T(8,128)}, f32[1,64,128]{2,1,0:T(8,128)}, f32[1,64,128]{2,1,0:T(8,128)}, f32[1,128,512]{2,1,0:T(8,128)}, f32[1,128,128]{2...) custom-call(bf16[1,128,512]{2,1,0:T(8,128)(2,1)} %q_hbm.1, ...), custom_call_target="tpu_custom_call" | custom-call | tf_op jit(solution)/shard_map/pallas_call | solution.py:549
  58.3 23.7 %shard_map.187 = (f32[1,128,512]{2,1,0:T(8,128)}, f32[1,64,128]{2,1,0:T(8,128)}, f32[1,64,128]{2,1,0:T(8,128)}, f32[1,128,512]{2,1,0:T(8,128)}, f32[1,128,128]{2...) custom-call(f32[1,128,512]{2,1,0:T(8,128)} %get-tuple-element.28.refs_0_, ...), custom_call_target="tpu_custom_call" | custom-call | tf_op jit(solution)/shard_map/pallas_call | solution.py:563

commit v3 on v2

--- a/solution.py
+++ b/solution.py
@@ -36,7 +36,7 @@
     kv_buf, kf, vf, q_st, q_t, s_buf, m_buf, l_buf, acc, gl_st, gl_t, delta_b,
     gy, dsc, ecx, w2x, dx, x_v, dtl_b, w_b, gym_b,
     cl_all, es_send, es_recv, es_out, ex_recv, fs_send, fs_recv, fs_out, fi_recv,
-    kg_send, kg_recv, ps_send, ps_recv, ps_out, pp_all, pd_all,
+    kg_send, kg_recv, gw_send, gr_send, ps_recv, ps_out, pp_all, pd_all,
     gq_o, gk_o, gv_o, gg_o, gw_o, gr_o, gdt_o, pf,
     in_sem, out_sem, kv_ss, kv_rs, cl_ss, cl_rs, es_ss, es_rs, ex_ss, ex_rs, fs_ss, fs_rs, fi_ss, fi_rs,
     kg_ss, kg_rs, p1_ss, p1_rs, p2_ss, p2_rs, pa_ss, pa_rs, pb_ss, pb_rs,
@@ -50,6 +50,9 @@
     base = z - par
     other = base + 1 - par
     chunk = lax.div(s, 2)
+    core = lax.rem(s, 2)
+    sibling = s + 1 - 2 * core
+    nchip = nseq // 2
     scale = 128 ** (-0.5)
 
     def rcopy(src, dst, ssem, rsem, **where):
@@ -97,16 +100,25 @@
 
     pl.semaphore_wait(barrier, 2 * (nseq - 1) + (ntp - 1) + (ndp - 1))
 
-    def kv_copy(d, p, to_seq, to_tp):
-        here = kv_buf.at[par, s]
-        return rcopy(here, here, kv_ss.at[d, p], kv_rs.at[par, s], seq=to_seq, tp=to_tp)
-
-    kv_copy(0, 0, s, other).start()
-    for d in range(1, nseq):
-        @pl.when(s + d < nseq)
+    def kv_copy(kind, at, p, j, **where):
+        here = kv_buf.at[p, j]
+        return rcopy(here, here, kv_ss.at[kind, at], kv_rs.at[p, j], **where)
+
+    def kv_along(d):
+        return kv_copy(0, d, par, s, seq=s + 2 * d)
+
+    def kv_partner(y):
+        return kv_copy(1, y, par, 2 * y + core, tp=other)
+
+    for d in range(1, nchip):
+        @pl.when(chunk + d < nchip)
         def _(d=d):
-            kv_copy(d, 0, s + d, base).start()
-            kv_copy(d, 1, s + d, base + 1).start()
+            kv_along(d).start()
+    kv_partner(chunk).start()
+
+    @pl.when(core == 0)
+    def _():
+        kv_copy(2, chunk, par, s, seq=sibling).start()
 
     row_i = lax.broadcasted_iota(jnp.int32, (rows, rows), 0)
     col_i = lax.broadcasted_iota(jnp.int32, (rows, rows), 1)
@@ -195,6 +207,14 @@
         w_b[p] = jnp.concatenate(ws, axis=1)
         dx[:, lanes] = mm_tn(jnp.concatenate(ws, axis=0), gym) + skip_row[:, lanes] * gp
 
+    for d in (1, 3, 2) if nchip == 4 else range(1, nchip):
+        @pl.when(chunk >= d)
+        def _(d=d):
+            y = chunk - d
+            kv_copy(0, 0, par, 2 * y + core, tp=other).wait_recv()
+            kv_partner(y).start()
+            kv_copy(2, y, par, 2 * y + core, seq=sibling).start()
+
     def wait_from(make, skip_self=True):
         for d in range(1, nseq):
             make(lax.rem(s + d, nseq)).wait_recv()
@@ -222,6 +242,19 @@
         es_out[i] = state.astype(BF16)
         send_back(es_out, ex_recv, ex_ss, ex_rs, i)
         state = es_recv[i].astype(F32) + jnp.exp(-cl_all[i, pl.ds(s, 1), :]) * state
+
+    def from_partner(y):
+        kv_copy(0, 0, 1 - par, 2 * y + core, tp=other).wait_recv()
+
+        @pl.when(jnp.logical_or(y < chunk, core == 0))
+        def _():
+            kv_copy(3, y, 1 - par, 2 * y + core, seq=sibling).start()
+
+    from_partner(chunk)
+    for d in (1, 3, 2) if nchip == 4 else range(1, nchip):
+        @pl.when(chunk >= d)
+        def _(d=d):
+            from_partner(chunk - d)
 
     loads[7].wait()
     for p in range(nq):
@@ -232,13 +265,11 @@
     acc[...] = jnp.zeros((nq * rows, 128), F32)
 
     def scores(i, carry):
-        for c in range(2):
-            j = 2 * i + c
+        @pl.when(jnp.logical_or(i < chunk, core == 1))
+        def _():
             for p in range(2):
-                @pl.when(jnp.logical_and(j <= s, jnp.logical_or(j != s, p != par)))
-                def _(p=p, j=j):
-                    slot = kv_buf.at[p, j]
-                    rcopy(slot, slot, kv_ss.at[0, 0], kv_rs.at[p, j], tp=other).wait_recv()
+                kv_copy(0, 0, p, 2 * i + 1 - core, tp=other).wait_recv()
+
         lo = jnp.concatenate([kv_buf[0, 2 * i], kv_buf[0, 2 * i + 1]], axis=1)
         hi = jnp.concatenate([kv_buf[1, 2 * i], kv_buf[1, 2 * i + 1]], axis=1)
         kk = jnp.concatenate([lo[:64], hi[:64]], axis=0)
@@ -306,7 +337,24 @@
     gyx = mm_nt(eb64, x_v[...] * gy[...], HIGH)
     dx[...] = dx[...] + dx_exit
     grad_w = mm_tn(m_sum.astype(BF16), read_v[...]) + mm(xw, exit_g)
-    ps_send[:rows, :] = grad_w.astype(BF16)
+    gw_send[...] = grad_w.astype(BF16)
+
+    part = 2 * rows // ntp
+
+    def p1_copy(send, o, odd):
+        return rcopy(send.at[pl.ds(part * o, part)], ps_recv.at[z], p1_ss.at[odd, o], p1_rs.at[z], tp=2 * o + odd)
+
+    def p1_start(send, odd):
+        for o in range(ntp // 2):
+            @pl.when(z != 2 * o + odd)
+            def _(o=o):
+                p1_copy(send, o, odd).start()
+
+            @pl.when(z == 2 * o + odd)
+            def _(o=o):
+                ps_recv[z] = send[part * o:part * o + part, :]
+
+    p1_start(gw_send, 1)
 
     wait_from(lambda j: rcopy(fs_recv.at[j], fs_recv.at[j], fs_ss.at[0], fs_rs.at[j], seq=j))
     state = jnp.zeros((64, 128), F32)
@@ -355,12 +403,6 @@
                 kg_send[p, 2 * i + c] = jnp.concatenate(
                     [gk[64 * p:64 * p + 64, 128 * c:128 * c + 128], gv[64 * p:64 * p + 64, 128 * c:128 * c + 128]], axis=0
                 )
-        for c in range(2):
-            j = 2 * i + c
-            for p in range(2):
-                @pl.when(jnp.logical_and(j <= s, jnp.logical_not(kg_mine(p, j))))
-                def _(p=p, j=j):
-                    kg_copy(p, j).start()
         return carry
 
     lax.fori_loop(0, chunk + 1, backward, 0)
@@ -372,17 +414,13 @@
     entry = fi_recv[...]
     gye = (gy[...] * ecx[...]).astype(BF16)
     grad_r = mm(m_sum.astype(BF16), write_v[...]) + mm(gye, entry)
-    ps_send[rows:, :] = grad_r.astype(BF16)
-    part = 2 * rows // ntp
-
-    def p1_copy(d):
-        to = lax.rem(z + d, ntp)
-        return rcopy(seq_block(ps_send, to, part), ps_recv.at[z], p1_ss.at[d], p1_rs.at[z], tp=to)
-
-    for d in range(1, ntp):
-        p1_copy(d).start()
-    own_part = pl.ds(pl.multiple_of(z * part, part), part)
-    ps_recv[z] = ps_send[own_part, :]
+    gr_send[...] = grad_r.astype(BF16)
+    p1_start(gr_send, 0)
+    for j in range(nseq):
+        for p in range(2):
+            @pl.when(jnp.logical_and(j <= s, jnp.logical_not(kg_mine(p, j))))
+            def _(p=p, j=j):
+                kg_copy(p, j).start()
 
     y_ent = mm_nt(read_v[...], entry) * ecx[...]
     q_sum = mm_nt(eb64, gy[...] * y_ent, HIGH)
@@ -421,15 +459,14 @@
 
     for d in range(1, ntp):
         j = lax.rem(z + d, ntp)
-        rcopy(ps_recv.at[j], ps_recv.at[j], p1_ss.at[0], p1_rs.at[j], tp=j).wait_recv()
+        rcopy(ps_recv.at[j], ps_recv.at[j], p1_ss.at[0, 0], p1_rs.at[j], tp=j).wait_recv()
     red = ps_recv[0].astype(F32)
     for j in range(1, ntp):
         red = red + ps_recv[j].astype(F32)
-    ps_out[own_part, :] = red.astype(BF16)
+    ps_out[z] = red.astype(BF16)
 
     def p2_copy(d):
-        here = seq_block(ps_out, z, part)
-        return rcopy(here, here, p2_ss.at[d], p2_rs.at[z], tp=lax.rem(z + d, ntp))
+        return rcopy(ps_out.at[z], ps_out.at[z], p2_ss.at[d], p2_rs.at[z], tp=lax.rem(z + d, ntp))
 
     for d in range(1, ntp):
         p2_copy(d).start()
@@ -470,19 +507,27 @@
 
     for d in range(1, ntp):
         j = lax.rem(z + d, ntp)
-        there = seq_block(ps_out, j, part)
-        rcopy(there, there, p2_ss.at[0], p2_rs.at[j], tp=j).wait_recv()
-    gw_o[...] = ps_out[:rows, :].astype(F32)
-    gr_o[...] = ps_out[rows:, :].astype(F32)
+        rcopy(ps_out.at[j], ps_out.at[j], p2_ss.at[0], p2_rs.at[j], tp=j).wait_recv()
+    for o in range(ntp // 2):
+        gw_o[part * o:part * o + part, :] = ps_out[2 * o + 1].astype(F32)
+        gr_o[part * o:part * o + part, :] = ps_out[2 * o].astype(F32)
     put(gw_o, gw_hbm.at[0])
     put(gr_o, gr_hbm.at[0])
 
-    kv_copy(0, 0, s, other).wait_send()
+    for d in range(1, nchip):
+        @pl.when(chunk + d < nchip)
+        def _(d=d):
+            kv_along(d).wait_send()
+    for y in range(nchip):
+        @pl.when(y <= chunk)
+        def _(y=y):
+            kv_partner(y).wait_send()
+
+        @pl.when(jnp.logical_or(y < chunk, jnp.logical_and(y == chunk, core == 0)))
+        def _(y=y):
+            kv_copy(2, y, par, 2 * y + core, seq=sibling).wait_send()
+            kv_copy(3, y, 1 - par, 2 * y + core, seq=sibling).wait_send()
     for d in range(1, nseq):
-        @pl.when(s + d < nseq)
-        def _(d=d):
-            kv_copy(d, 0, s + d, base).wait_send()
-            kv_copy(d, 1, s + d, base + 1).wait_send()
         cl_copy(d, lax.rem(s + d, nseq)).wait_send()
         es_copy(d).wait_send()
         fs_copy(d).wait_send()
@@ -497,8 +542,12 @@
             def _(p=p, i=i):
                 kg_copy(p, i).wait_send()
     for d in range(1, ntp):
-        p1_copy(d).wait_send()
         p2_copy(d).wait_send()
+    for o in range(ntp // 2):
+        for odd, send in ((1, gw_send), (0, gr_send)):
+            @pl.when(z != 2 * o + odd)
+            def _(o=o, odd=odd, send=send):
+                p1_copy(send, o, odd).wait_send()
     for d in range(1, ndp):
         pb_copy(d).wait_send()
     for copy in outs:
@@ -536,14 +585,15 @@
         vm((wide, 128), BF16), vm((nseq, 64, 128), BF16), vm((nseq, 64, 128), BF16), vm((wide, 128), BF16),
         vm((wide, 128), BF16), vm((nseq, 64, 128), BF16), vm((nseq, 64, 128), BF16), vm((wide, 128), BF16),
         vm((2, nseq, 128, rows), BF16), vm((2, nseq, 128, rows), BF16),
-        vm((2 * rows, 128), BF16), vm((ntp, 2 * rows // ntp, 128), BF16), vm((2 * rows, 128), BF16),
+        vm((rows, 128), BF16), vm((rows, 128), BF16),
+        vm((ntp, 2 * rows // ntp, 128), BF16), vm((ntp, 2 * rows // ntp, 128), BF16),
         vm((nseq, nheads, 128)), vm((ndp, nheads, 128)),
         vm((rows, wide)), vm((64, rows)), vm((64, rows)), vm((rows, wide)), vm((rows, 128)), vm((rows, 128)),
         vm((nheads, rows)), vm((nheads, 128)),
-        dma((8,)), dma((8,)), dma((nseq, 2)), dma((2, nseq)), dma((nseq,)), dma((nseq,)),
+        dma((8,)), dma((8,)), dma((4, max(nseq // 2, 4))), dma((2, nseq)), dma((nseq,)), dma((nseq,)),
         dma((nseq,)), dma((nseq,)), dma((nseq,)), dma((nseq,)),
         dma((nseq,)), dma((nseq,)), dma((nseq,)), dma((nseq,)),
-        dma((2, nseq)), dma((2, nseq)), dma((ntp,)), dma((ntp,)), dma((ntp,)), dma((ntp,)),
+        dma((2, nseq)), dma((2, nseq)), dma((2, ntp)), dma((ntp,)), dma((ntp,)), dma((ntp,)),
         dma((nseq,)), dma((nseq,)), dma((ndp,)), dma((ndp,)),
     ]
     results = pl.pallas_call(
@@ -565,7 +615,7 @@
         out_shape=tuple([jax.ShapeDtypeStruct(o, F32) for o in outs[:7]] + [per_head] * 3),
         in_specs=[any_spec] * 8,
         out_specs=tuple([any_spec] * 7 + [smem_spec] * 3),
-        scratch_shapes=[dma((8,)), pltpu.SMEM((nheads, 128), F32)],
+        scratch_shapes=[dma((8,)), dma((8,)), pltpu.SMEM((nheads, 128), F32)] + [vm(o) for o in outs[:7]],
         compiler_params=pltpu.CompilerParams(vmem_limit_bytes=VMEM),
     )(*results)
     return (
@@ -574,16 +624,21 @@
 
 
 def write_out(nheads, *refs):
-    sources, targets, (sems, small) = refs[:8], refs[8:18], refs[18:]
-    copies = [pltpu.make_async_copy(sources[7], small, sems.at[7])]
-    copies += [pltpu.make_async_copy(a, b, sems.at[i]) for i, (a, b) in enumerate(zip(sources[:7], targets[:7]))]
-    for copy in copies:
+    sources, targets, (load_sem, store_sem, small), staged = refs[:8], refs[8:18], refs[18:21], refs[21:]
+    loads = [pltpu.make_async_copy(sources[7], small, load_sem.at[7])]
+    loads += [pltpu.make_async_copy(sources[i], staged[i], load_sem.at[i]) for i in range(7)]
+    for copy in loads:
         copy.start()
-    copies[0].wait()
+    stores = []
+    for i in range(7):
+        loads[1 + i].wait()
+        stores.append(pltpu.make_async_copy(staged[i], targets[i], store_sem.at[i]))
+        stores[i].start()
+    loads[0].wait()
     for h in range(nheads):
         for i in range(3):
             targets[7 + i][h] = small[h, i]
-    for copy in copies[1:]:
+    for copy in stores:
         copy.wait()
 
 

time: 82.3 us -> 55 us (0.67)
  the two profiles are of different devices: /device:TPU:8 before, /device:TPU:1 now
where the time goes in v3:
time: 55 us; the launch traced here: 54.1 us
  Pallas kernels  53.4 us (97%)
  between operations  0.65 us (1%)
    pallas_call x1, Pallas kernels, body(): pl.pallas_call(functools.partial(kernel, dims), out_shape=tuple((jax.Shap...  50.9 us
    pallas_call x1, Pallas kernels, body(): pl.pallas_call(functools.partial(write_out, nheads), out_shape=tuple([jax...  2.49 us

profile of v3, /device:TPU:1, one launch (start us, length us, event | category | flops | bytes accessed | tf_op | source)
XLA Modules:
  0.0 54.1 jit_solution(8564523091975579958)
XLA Ops:
  0.6 50.9 %shard_map.186 = (f32[1,128,512]{2,1,0:T(8,128)}, f32[1,64,128]{2,1,0:T(8,128)}, f32[1,64,128]{2,1,0:T(8,128)}, f32[1,128,512]{2,1,0:T(8,128)}, f32[1,128,128]{2...) custom-call(bf16[1,128,512]{2,1,0:T(8,128)(2,1)} %q_hbm.1, ...), custom_call_target="tpu_custom_call" | custom-call | tf_op jit(solution)/shard_map/pallas_call | solution.py:599
  51.6 2.5 %shard_map.187 = (f32[1,128,512]{2,1,0:T(8,128)}, f32[1,64,128]{2,1,0:T(8,128)}, f32[1,64,128]{2,1,0:T(8,128)}, f32[1,128,512]{2,1,0:T(8,128)}, f32[1,128,128]{2...) custom-call(f32[1,128,512]{2,1,0:T(8,128)} %get-tuple-element.28.refs_0_, ...), custom_call_target="tpu_custom_call" | custom-call | tf_op jit(solution)/shard_map/pallas_call | solution.py:613

commit v4 on v3

--- a/solution.py
+++ b/solution.py
@@ -36,10 +36,10 @@
     kv_buf, kf, vf, q_st, q_t, s_buf, m_buf, l_buf, acc, gl_st, gl_t, delta_b,
     gy, dsc, ecx, w2x, dx, x_v, dtl_b, w_b, gym_b,
     cl_all, es_send, es_recv, es_out, ex_recv, fs_send, fs_recv, fs_out, fi_recv,
-    kg_send, kg_recv, gw_send, gr_send, ps_recv, ps_out, pp_all, pd_all,
+    kg_send, kg_sib, kg_recv, gw_send, gr_send, ps_recv, ps_out, pp_all, pd_all,
     gq_o, gk_o, gv_o, gg_o, gw_o, gr_o, gdt_o, pf,
-    in_sem, out_sem, kv_ss, kv_rs, cl_ss, cl_rs, es_ss, es_rs, ex_ss, ex_rs, fs_ss, fs_rs, fi_ss, fi_rs,
-    kg_ss, kg_rs, p1_ss, p1_rs, p2_ss, p2_rs, pa_ss, pa_rs, pb_ss, pb_rs,
+    far_sem, in_sem, out_sem, kv_ss, kv_rs, cl_ss, cl_rs, es_ss, es_rs, ex_ss, ex_rs, fs_ss, fs_rs, fi_ss, fi_rs,
+    sib_ss, sib_rs, kg_ss, kg_rs, p1_ss, p1_rs, p2_ss, p2_rs, pa_ss, pa_rs, pb_ss, pb_rs,
 ):
     nseq, ntp, ndp, nheads, nq = dims
     rows = 128
@@ -84,7 +84,7 @@
         to = lax.rem(s + d, nseq)
         pl.semaphore_signal(barrier, inc=1, device_id={"seq": to, "tp": z}, device_id_type=MESH)
         pl.semaphore_signal(barrier, inc=1, device_id={"seq": to, "tp": other}, device_id_type=MESH)
-    for d in range(1, ntp):
+    for d in (1, ntp - 1):
         pl.semaphore_signal(barrier, inc=1, device_id={"tp": lax.rem(z + d, ntp)}, device_id_type=MESH)
     for d in range(1, ndp):
         pl.semaphore_signal(barrier, inc=1, device_id={"dp": lax.rem(x + d, ndp)}, device_id_type=MESH)
@@ -98,7 +98,19 @@
         kv_buf[0, s + 1] = jnp.zeros((rows, 128), BF16)
         kv_buf[1, s + 1] = jnp.zeros((rows, 128), BF16)
 
-    pl.semaphore_wait(barrier, 2 * (nseq - 1) + (ntp - 1) + (ndp - 1))
+    pl.semaphore_wait(barrier, 2 * (nseq - 1) + 2 + (ndp - 1))
+
+    rounds = [d for d in (1, 2, 4, 8) if d < ntp // 2]
+
+    def tell(r):
+        for d in (rounds[r], ntp - rounds[r]):
+            pl.semaphore_signal(far_sem.at[r], inc=1, device_id={"tp": lax.rem(z + d, ntp)}, device_id_type=MESH)
+
+    def hear(r):
+        pl.semaphore_wait(far_sem.at[r], 2)
+
+    if rounds:
+        tell(0)
 
     def kv_copy(kind, at, p, j, **where):
         here = kv_buf.at[p, j]
@@ -182,8 +194,6 @@
             copy(d).start()
         recv[s] = send[pl.ds(pl.multiple_of(s * 64, 64), 64), :]
         return copy
-
-    es_copy = all_to_all(es_send, es_recv, es_ss, es_rs)
 
     loads[6].wait()
     cb = mm_nt(read_v[...], write_v[...])
@@ -207,6 +217,10 @@
         w_b[p] = jnp.concatenate(ws, axis=1)
         dx[:, lanes] = mm_tn(jnp.concatenate(ws, axis=0), gym) + skip_row[:, lanes] * gp
 
+    if len(rounds) > 1:
+        hear(0)
+        tell(1)
+
     for d in (1, 3, 2) if nchip == 4 else range(1, nchip):
         @pl.when(chunk >= d)
         def _(d=d):
@@ -215,33 +229,11 @@
             kv_partner(y).start()
             kv_copy(2, y, par, 2 * y + core, seq=sibling).start()
 
+    es_copy = all_to_all(es_send, es_recv, es_ss, es_rs)
+
     def wait_from(make, skip_self=True):
         for d in range(1, nseq):
             make(lax.rem(s + d, nseq)).wait_recv()
-
-    wait_from(lambda j: rcopy(cl_all.at[j], cl_all.at[j], cl_ss.at[0], cl_rs.at[j], seq=j))
-    wait_from(lambda j: rcopy(es_recv.at[j], es_recv.at[j], es_ss.at[0], es_rs.at[j], seq=j))
-
-    def back_copy(out, recv, ss, rs, i):
-        here = seq_block(recv, s, 64)
-        return rcopy(out.at[i], here, ss.at[i], rs.at[s], seq=i)
-
-    own_head = pl.ds(pl.multiple_of(s * 64, 64), 64)
-
-    def send_back(out, recv, ss, rs, i):
-        @pl.when(s != i)
-        def _():
-            back_copy(out, recv, ss, rs, i).start()
-
-        @pl.when(s == i)
-        def _():
-            recv[own_head, :] = out[i]
-
-    state = jnp.zeros((64, 128), F32)
-    for i in reversed(range(nseq)):
-        es_out[i] = state.astype(BF16)
-        send_back(es_out, ex_recv, ex_ss, ex_rs, i)
-        state = es_recv[i].astype(F32) + jnp.exp(-cl_all[i, pl.ds(s, 1), :]) * state
 
     def from_partner(y):
         kv_copy(0, 0, 1 - par, 2 * y + core, tp=other).wait_recv()
@@ -255,6 +247,10 @@
         @pl.when(chunk >= d)
         def _(d=d):
             from_partner(chunk - d)
+
+    if len(rounds) > 2:
+        hear(1)
+        tell(2)
 
     loads[7].wait()
     for p in range(nq):
@@ -287,6 +283,30 @@
         return carry
 
     lax.fori_loop(0, chunk + 1, scores, 0)
+    wait_from(lambda j: rcopy(cl_all.at[j], cl_all.at[j], cl_ss.at[0], cl_rs.at[j], seq=j))
+    wait_from(lambda j: rcopy(es_recv.at[j], es_recv.at[j], es_ss.at[0], es_rs.at[j], seq=j))
+
+    def back_copy(out, recv, ss, rs, i):
+        here = seq_block(recv, s, 64)
+        return rcopy(out.at[i], here, ss.at[i], rs.at[s], seq=i)
+
+    own_head = pl.ds(pl.multiple_of(s * 64, 64), 64)
+
+    def send_back(out, recv, ss, rs, i):
+        @pl.when(s != i)
+        def _():
+            back_copy(out, recv, ss, rs, i).start()
+
+        @pl.when(s == i)
+        def _():
+            recv[own_head, :] = out[i]
+
+    state = jnp.zeros((64, 128), F32)
+    for i in reversed(range(nseq)):
+        es_out[i] = state.astype(BF16)
+        send_back(es_out, ex_recv, ex_ss, ex_rs, i)
+        state = es_recv[i].astype(F32) + jnp.exp(-cl_all[i, pl.ds(s, 1), :]) * state
+
     m_buf[...] = jnp.broadcast_to(jnp.max(m_buf[...], axis=1, keepdims=True), (nq * rows, 128))
 
     def weights(i, carry):
@@ -330,6 +350,13 @@
         row_r = jnp.where(head_i == 2 * p, rs[0:1, :rows], row_r)
         row_r = jnp.where(head_i == 2 * p + 1, rs[0:1, rows:], row_r)
 
+    wait_from(lambda j: rcopy(fs_recv.at[j], fs_recv.at[j], fs_ss.at[0], fs_rs.at[j], seq=j))
+    state = jnp.zeros((64, 128), F32)
+    for i in range(nseq):
+        fs_out[i] = state.astype(BF16)
+        send_back(fs_out, fi_recv, fi_ss, fi_rs, i)
+        state = fs_recv[i].astype(F32) + jnp.exp(-cl_all[i, pl.ds(s, 1), :]) * state
+
     wait_from(lambda j: rcopy(seq_block(ex_recv, j, 64), seq_block(ex_recv, j, 64), ex_ss.at[0], ex_rs.at[j], seq=j))
     exit_g = ex_recv[...]
     dx_exit = mm_nt(write_v[...], exit_g) * w2x[...]
@@ -354,14 +381,9 @@
             def _(o=o):
                 ps_recv[z] = send[part * o:part * o + part, :]
 
+    if rounds:
+        hear(len(rounds) - 1)
     p1_start(gw_send, 1)
-
-    wait_from(lambda j: rcopy(fs_recv.at[j], fs_recv.at[j], fs_ss.at[0], fs_rs.at[j], seq=j))
-    state = jnp.zeros((64, 128), F32)
-    for i in range(nseq):
-        fs_out[i] = state.astype(BF16)
-        send_back(fs_out, fi_recv, fi_ss, fi_rs, i)
-        state = fs_recv[i].astype(F32) + jnp.exp(-cl_all[i, pl.ds(s, 1), :]) * state
 
     for p in range(nq):
         r = slice(rows * p, rows * p + rows)
@@ -373,14 +395,16 @@
         )
     acc[...] = jnp.zeros((nq * rows, 128), F32)
 
-    def kg_copy(p, j):
+    def sib_copy(i):
         return rcopy(
-            kg_send.at[p, j], kg_recv.at[par, s],
-            kg_ss.at[p, j], kg_rs.at[par, s], seq=j, tp=base + p,
+            kg_send.at[1 - core, pl.ds(2 * i, 2)], kg_sib.at[i], sib_ss.at[i], sib_rs.at[i], seq=sibling
         )
 
-    def kg_mine(p, j):
-        return jnp.logical_and(j == s, p == par)
+    def kg_copy(j):
+        return rcopy(kg_send.at[core, j], kg_recv.at[par, chunk], kg_ss.at[j], kg_rs.at[par, chunk], seq=j, tp=base + core)
+
+    def kg_mine(j):
+        return jnp.logical_and(j == s, par == core)
 
     def backward(i, carry):
         kk = kf[i]
@@ -403,10 +427,10 @@
                 kg_send[p, 2 * i + c] = jnp.concatenate(
                     [gk[64 * p:64 * p + 64, 128 * c:128 * c + 128], gv[64 * p:64 * p + 64, 128 * c:128 * c + 128]], axis=0
                 )
+        sib_copy(i).start()
         return carry
 
     lax.fori_loop(0, chunk + 1, backward, 0)
-    kg_recv[par, s] = kg_send[par, s]
     for p in range(nq):
         gq_o[:, 128 * p:128 * p + 128] = acc[128 * p:128 * p + 128, :] * scale
     put(gq_o, gq_hbm.at[0])
@@ -416,11 +440,24 @@
     grad_r = mm(m_sum.astype(BF16), write_v[...]) + mm(gye, entry)
     gr_send[...] = grad_r.astype(BF16)
     p1_start(gr_send, 0)
-    for j in range(nseq):
-        for p in range(2):
-            @pl.when(jnp.logical_and(j <= s, jnp.logical_not(kg_mine(p, j))))
-            def _(p=p, j=j):
-                kg_copy(p, j).start()
+
+    def kg_join(i, carry):
+        sib_copy(i).wait()
+        both = pl.ds(2 * i, 2)
+        kg_send[core, both] = (kg_send[core, both].astype(F32) + kg_sib[i].astype(F32)).astype(BF16)
+        for c in range(2):
+            j = 2 * i + c
+
+            @pl.when(jnp.logical_not(kg_mine(j)))
+            def _(j=j):
+                kg_copy(j).start()
+        return carry
+
+    lax.fori_loop(0, chunk + 1, kg_join, 0)
+
+    @pl.when(par == core)
+    def _():
+        kg_recv[par, chunk] = kg_send[core, s]
 
     y_ent = mm_nt(read_v[...], entry) * ecx[...]
     q_sum = mm_nt(eb64, gy[...] * y_ent, HIGH)
@@ -483,14 +520,14 @@
     for d in range(1, ndp):
         pb_copy(d).start()
 
-    def kg_add(j, total):
+    def kg_add(y, total):
         for p in range(2):
-            @pl.when(jnp.logical_not(kg_mine(p, j)))
+            @pl.when(jnp.logical_or(y != chunk, jnp.logical_or(p != par, par != core)))
             def _(p=p):
-                rcopy(kg_recv.at[p, j], kg_recv.at[p, j], kg_ss.at[0, 0], kg_rs.at[p, j], tp=other).wait_recv()
-        return total + kg_recv[0, j].astype(F32) + kg_recv[1, j].astype(F32)
-
-    kg = lax.fori_loop(s, nseq, kg_add, jnp.zeros((rows, 128), F32))
+                rcopy(kg_recv.at[p, y], kg_recv.at[p, y], kg_ss.at[0], kg_rs.at[p, y], tp=other).wait_recv()
+        return total + kg_recv[0, y].astype(F32) + kg_recv[1, y].astype(F32)
+
+    kg = lax.fori_loop(chunk, nchip, kg_add, jnp.zeros((rows, 128), F32))
     gk_o[...] = kg[:64]
     gv_o[...] = kg[64:]
     put(gk_o, gk_hbm.at[0])
@@ -537,10 +574,10 @@
         def _(i=i):
             back_copy(es_out, ex_recv, ex_ss, ex_rs, i).wait_send()
             back_copy(fs_out, fi_recv, fi_ss, fi_rs, i).wait_send()
-        for p in range(2):
-            @pl.when(jnp.logical_and(i <= s, jnp.logical_not(kg_mine(p, i))))
-            def _(p=p, i=i):
-                kg_copy(p, i).wait_send()
+
+        @pl.when(jnp.logical_and(i <= 2 * chunk + 1, jnp.logical_not(kg_mine(i))))
+        def _(i=i):
+            kg_copy(i).wait_send()
     for d in range(1, ntp):
         p2_copy(d).wait_send()
     for o in range(ntp // 2):
@@ -584,16 +621,16 @@
         vm((nseq, nheads, 128)),
         vm((wide, 128), BF16), vm((nseq, 64, 128), BF16), vm((nseq, 64, 128), BF16), vm((wide, 128), BF16),
         vm((wide, 128), BF16), vm((nseq, 64, 128), BF16), vm((nseq, 64, 128), BF16), vm((wide, 128), BF16),
-        vm((2, nseq, 128, rows), BF16), vm((2, nseq, 128, rows), BF16),
+        vm((2, nseq, 128, rows), BF16), vm((nseq // 2, 2, 128, rows), BF16), vm((2, nseq // 2, 128, rows), BF16),
         vm((rows, 128), BF16), vm((rows, 128), BF16),
         vm((ntp, 2 * rows // ntp, 128), BF16), vm((ntp, 2 * rows // ntp, 128), BF16),
         vm((nseq, nheads, 128)), vm((ndp, nheads, 128)),
         vm((rows, wide)), vm((64, rows)), vm((64, rows)), vm((rows, wide)), vm((rows, 128)), vm((rows, 128)),
         vm((nheads, rows)), vm((nheads, 128)),
-        dma((8,)), dma((8,)), dma((4, max(nseq // 2, 4))), dma((2, nseq)), dma((nseq,)), dma((nseq,)),
+        pltpu.SemaphoreType.REGULAR((4,)), dma((8,)), dma((8,)), dma((4, max(nseq // 2, 4))), dma((2, nseq)), dma((nseq,)), dma((nseq,)),
         dma((nseq,)), dma((nseq,)), dma((nseq,)), dma((nseq,)),
         dma((nseq,)), dma((nseq,)), dma((nseq,)), dma((nseq,)),
-        dma((2, nseq)), dma((2, nseq)), dma((2, ntp)), dma((ntp,)), dma((ntp,)), dma((ntp,)),
+        dma((nseq // 2,)), dma((nseq // 2,)), dma((nseq,)), dma((2, nseq // 2)), dma((2, ntp)), dma((ntp,)), dma((ntp,)), dma((ntp,)),
         dma((nseq,)), dma((nseq,)), dma((ndp,)), dma((ndp,)),
     ]
     results = pl.pallas_call(

time: 55 us -> 51 us (0.927); the launches traced: 54.1 us -> 50.7 us
  Pallas kernels: 53.4 us -> 50 us
    pallas_call x1, Pallas kernels: 50.9 us -> 47.5 us  [body(): pl.pallas_call(functools.partial(kernel, dims), out_shape=tuple((jax.Shap...]
where the time goes in v4:
time: 51 us; the launch traced here: 50.7 us
  Pallas kernels  50 us (98%)
  between operations  0.65 us (1%)
    pallas_call x1, Pallas kernels, body(): pl.pallas_call(functools.partial(kernel, dims), out_shape=tuple((jax.Shap...  47.5 us
    pallas_call x1, Pallas kernels, body(): pl.pallas_call(functools.partial(write_out, nheads), out_shape=tuple([jax...  2.49 us

profile of v4, /device:TPU:1, one launch (start us, length us, event | category | flops | bytes accessed | tf_op | source)
XLA Modules:
  0.0 50.7 jit_solution(17327874522640043402)
XLA Ops:
  0.6 47.5 %shard_map.186 = (f32[1,128,512]{2,1,0:T(8,128)}, f32[1,64,128]{2,1,0:T(8,128)}, f32[1,64,128]{2,1,0:T(8,128)}, f32[1,128,512]{2,1,0:T(8,128)}, f32[1,128,128]{2...) custom-call(bf16[1,128,512]{2,1,0:T(8,128)(2,1)} %q_hbm.1, ...), custom_call_target="tpu_custom_call" | custom-call | tf_op jit(solution)/shard_map/pallas_call | solution.py:636
  48.2 2.5 %shard_map.187 = (f32[1,128,512]{2,1,0:T(8,128)}, f32[1,64,128]{2,1,0:T(8,128)}, f32[1,64,128]{2,1,0:T(8,128)}, f32[1,128,512]{2,1,0:T(8,128)}, f32[1,128,128]{2...) custom-call(f32[1,128,512]{2,1,0:T(8,128)} %get-tuple-element.28.refs_0_, ...), custom_call_target="tpu_custom_call" | custom-call | tf_op jit(solution)/shard_map/pallas_call | solution.py:650

commit v5 on v4

--- a/solution.py
+++ b/solution.py
@@ -12,7 +12,7 @@
 F32 = jnp.float32
 BF16 = jnp.bfloat16
 NEG_FILL = -1e30
-VMEM = 60 * 1024 * 1024
+VMEM = 40 * 1024 * 1024
 
 
 def mm(a, b, precision=None):
@@ -31,15 +31,14 @@
     dims,
     q_hbm, k_hbm, v_hbm, gate_hbm, write_hbm, read_hbm, dt_hbm, cot_hbm,
     alog_s, skip_s, bias_s,
-    gq_hbm, gk_hbm, gv_hbm, gg_hbm, gw_hbm, gr_hbm, gdt_hbm, pf_hbm,
+    gq_o, gk_o, gv_o, gg_o, gw_o, gr_o, gdt_o, pf,
     q_v, k_v, v_v, gate_v, write_v, read_v, dt_v, cot_v,
     kv_buf, kf, vf, q_st, q_t, s_buf, m_buf, l_buf, acc, gl_st, gl_t, delta_b,
-    gy, dsc, ecx, w2x, dx, x_v, dtl_b, w_b, gym_b,
+    gy, dsc, ecx, w2x, dx, x_v, dtl_b, w_b, gym_b, gye_b, gr_part,
     cl_all, es_send, es_recv, es_out, ex_recv, fs_send, fs_recv, fs_out, fi_recv,
-    kg_send, kg_sib, kg_recv, gw_send, gr_send, ps_recv, ps_out, pp_all, pd_all,
-    gq_o, gk_o, gv_o, gg_o, gw_o, gr_o, gdt_o, pf,
-    far_sem, in_sem, out_sem, kv_ss, kv_rs, cl_ss, cl_rs, es_ss, es_rs, ex_ss, ex_rs, fs_ss, fs_rs, fi_ss, fi_rs,
-    sib_ss, sib_rs, kg_ss, kg_rs, p1_ss, p1_rs, p2_ss, p2_rs, pa_ss, pa_rs, pb_ss, pb_rs,
+    kg_send, kg_sib, kg_recv, kg_sum, kg_give, kg_take, gw_send, gr_send, ps_recv, ps_out, pp_all, pd_all,
+    far_sem, in_sem, kv_ss, kv_rs, cl_ss, cl_rs, es_ss, es_rs, ex_ss, ex_rs, fs_ss, fs_rs, fi_ss, fi_rs,
+    sib_ss, sib_rs, kg_ss, kg_rs, kx_ss, kx_rs, p1_ss, p1_rs, p2_ss, p2_rs, pa_ss, pa_rs, pb_ss, pb_rs,
 ):
     nseq, ntp, ndp, nheads, nq = dims
     rows = 128
@@ -63,13 +62,6 @@
     def seq_block(ref, i, n):
         return ref.at[pl.ds(pl.multiple_of(i * n, n), n)]
 
-    outs = []
-
-    def put(src, dst):
-        copy = pltpu.make_async_copy(src, dst, out_sem.at[len(outs)])
-        copy.start()
-        outs.append(copy)
-
     loads = []
     for at, (src, dst) in enumerate((
         (k_hbm.at[0], k_v), (v_hbm.at[0], v_v), (dt_hbm.at[0], dt_v), (gate_hbm.at[0], gate_v),
@@ -122,7 +114,7 @@
     def kv_partner(y):
         return kv_copy(1, y, par, 2 * y + core, tp=other)
 
-    for d in range(1, nchip):
+    for d in (2, 3, 1) if nchip == 4 else range(1, nchip):
         @pl.when(chunk + d < nchip)
         def _(d=d):
             kv_along(d).start()
@@ -184,6 +176,7 @@
     dsc[...] = cot * sig * (1.0 + gate * (1.0 - sig))
     loads[5].wait()
     gye = (gy[...] * ecx[...]).astype(BF16)
+    gye_b[...] = gye
     es_send[...] = mm_tn(gye, read_v[...]).astype(BF16)
 
     def all_to_all(send, recv, ss, rs):
@@ -242,11 +235,12 @@
         def _():
             kv_copy(3, y, 1 - par, 2 * y + core, seq=sibling).start()
 
+    def visited(turn):
+        if nchip != 4:
+            return chunk - turn
+        return jnp.where(turn < 2, chunk - turn, turn - 2)
+
     from_partner(chunk)
-    for d in (1, 3, 2) if nchip == 4 else range(1, nchip):
-        @pl.when(chunk >= d)
-        def _(d=d):
-            from_partner(chunk - d)
 
     if len(rounds) > 2:
         hear(1)
@@ -260,7 +254,13 @@
     l_buf[...] = jnp.zeros((nq * rows, 128), F32)
     acc[...] = jnp.zeros((nq * rows, 128), F32)
 
-    def scores(i, carry):
+    def scores(turn, carry):
+        i = visited(turn)
+
+        @pl.when(turn < chunk)
+        def _():
+            from_partner(visited(turn + 1))
+
         @pl.when(jnp.logical_or(i < chunk, core == 1))
         def _():
             for p in range(2):
@@ -365,6 +365,7 @@
     dx[...] = dx[...] + dx_exit
     grad_w = mm_tn(m_sum.astype(BF16), read_v[...]) + mm(xw, exit_g)
     gw_send[...] = grad_w.astype(BF16)
+    gr_part[...] = mm(m_sum.astype(BF16), write_v[...])
 
     part = 2 * rows // ntp
 
@@ -401,10 +402,7 @@
         )
 
     def kg_copy(j):
-        return rcopy(kg_send.at[core, j], kg_recv.at[par, chunk], kg_ss.at[j], kg_rs.at[par, chunk], seq=j, tp=base + core)
-
-    def kg_mine(j):
-        return jnp.logical_and(j == s, par == core)
+        return rcopy(kg_send.at[core, j], kg_recv.at[core, chunk], kg_ss.at[j], kg_rs.at[core, chunk], seq=j)
 
     def backward(i, carry):
         kk = kf[i]
@@ -431,13 +429,9 @@
         return carry
 
     lax.fori_loop(0, chunk + 1, backward, 0)
-    for p in range(nq):
-        gq_o[:, 128 * p:128 * p + 128] = acc[128 * p:128 * p + 128, :] * scale
-    put(gq_o, gq_hbm.at[0])
     wait_from(lambda j: rcopy(seq_block(fi_recv, j, 64), seq_block(fi_recv, j, 64), fi_ss.at[0], fi_rs.at[j], seq=j))
     entry = fi_recv[...]
-    gye = (gy[...] * ecx[...]).astype(BF16)
-    grad_r = mm(m_sum.astype(BF16), write_v[...]) + mm(gye, entry)
+    grad_r = gr_part[...] + mm(gye_b[...], entry)
     gr_send[...] = grad_r.astype(BF16)
     p1_start(gr_send, 0)
 
@@ -448,17 +442,17 @@
         for c in range(2):
             j = 2 * i + c
 
-            @pl.when(jnp.logical_not(kg_mine(j)))
+            @pl.when(j != s)
             def _(j=j):
                 kg_copy(j).start()
         return carry
 
     lax.fori_loop(0, chunk + 1, kg_join, 0)
 
-    @pl.when(par == core)
-    def _():
-        kg_recv[par, chunk] = kg_send[core, s]
-
+    kg_recv[core, chunk] = kg_send[core, s]
+
+    for p in range(nq):
+        gq_o[0, :, 128 * p:128 * p + 128] = acc[128 * p:128 * p + 128, :] * scale
     y_ent = mm_nt(read_v[...], entry) * ecx[...]
     q_sum = mm_nt(eb64, gy[...] * y_ent, HIGH)
     for p in range(nheads // 2):
@@ -466,8 +460,7 @@
         xp = x_v[:, lanes]
         xm = jnp.concatenate([jnp.where(lane_lo, xp, 0.0), jnp.where(lane_lo, 0.0, xp)], axis=0).astype(BF16)
         y = mm(w_b[p], xm) + y_ent[:, lanes] + skip_row[:, lanes] * xp
-        gg_o[:, lanes] = dsc[:, lanes] * y
-    put(gg_o, gg_hbm.at[0])
+        gg_o[0, :, lanes] = dsc[:, lanes] * y
 
     es_prod = exit_g.astype(F32) * entry.astype(F32)
     c_h = jnp.sum(mm(eb64, es_prod, HIGH), axis=1, keepdims=True) * jnp.exp(-cum_last)
@@ -476,8 +469,7 @@
     drate = mm(col_r - row_r - q_sum, tail, HIGH) - mm(r_s, before, HIGH) - c_h
     ddt = (col_r + r_s) / dt + drate * ea
     draw = ddt * sig_z
-    gdt_o[...] = draw
-    put(gdt_o, gdt_hbm.at[0])
+    gdt_o[0] = draw
 
     lane8 = lax.broadcasted_iota(jnp.int32, (nheads, 128), 1)
     pp_all[s] = jnp.where(
@@ -521,17 +513,23 @@
         pb_copy(d).start()
 
     def kg_add(y, total):
-        for p in range(2):
-            @pl.when(jnp.logical_or(y != chunk, jnp.logical_or(p != par, par != core)))
-            def _(p=p):
-                rcopy(kg_recv.at[p, y], kg_recv.at[p, y], kg_ss.at[0], kg_rs.at[p, y], tp=other).wait_recv()
-        return total + kg_recv[0, y].astype(F32) + kg_recv[1, y].astype(F32)
-
-    kg = lax.fori_loop(chunk, nchip, kg_add, jnp.zeros((rows, 128), F32))
-    gk_o[...] = kg[:64]
-    gv_o[...] = kg[64:]
-    put(gk_o, gk_hbm.at[0])
-    put(gv_o, gv_hbm.at[0])
+        for c in range(2):
+            @pl.when(jnp.logical_or(y != chunk, core != c))
+            def _(c=c):
+                rcopy(kg_recv.at[c, y], kg_recv.at[c, y], kg_ss.at[0], kg_rs.at[c, y], tp=other).wait_recv()
+        return tuple(total[c] + kg_recv[c, y].astype(F32) for c in range(2))
+
+    blank = jnp.zeros((128, rows), F32)
+    half = lax.fori_loop(chunk, nchip, kg_add, (blank, blank))
+    for c in range(2):
+        kg_sum[c] = half[c]
+    kg_give[...] = kg_sum[1 - par].astype(BF16)
+    kx_copy = rcopy(kg_give, kg_take, kx_ss, kx_rs, tp=other)
+    kx_copy.start()
+    kx_copy.wait()
+    kg = kg_sum[par] + kg_take[...].astype(F32)
+    gk_o[0] = kg[:64]
+    gv_o[0] = kg[64:]
 
     for d in range(1, ndp):
         j = lax.rem(x + d, ndp)
@@ -540,16 +538,13 @@
     for j in range(1, ndp):
         pd = pd + pd_all[j]
     pf[...] = pd
-    put(pf, pf_hbm)
 
     for d in range(1, ntp):
         j = lax.rem(z + d, ntp)
         rcopy(ps_out.at[j], ps_out.at[j], p2_ss.at[0], p2_rs.at[j], tp=j).wait_recv()
     for o in range(ntp // 2):
-        gw_o[part * o:part * o + part, :] = ps_out[2 * o + 1].astype(F32)
-        gr_o[part * o:part * o + part, :] = ps_out[2 * o].astype(F32)
-    put(gw_o, gw_hbm.at[0])
-    put(gr_o, gr_hbm.at[0])
+        gw_o[0, part * o:part * o + part, :] = ps_out[2 * o + 1].astype(F32)
+        gr_o[0, part * o:part * o + part, :] = ps_out[2 * o].astype(F32)
 
     for d in range(1, nchip):
         @pl.when(chunk + d < nchip)
@@ -575,7 +570,7 @@
             back_copy(es_out, ex_recv, ex_ss, ex_rs, i).wait_send()
             back_copy(fs_out, fi_recv, fi_ss, fi_rs, i).wait_send()
 
-        @pl.when(jnp.logical_and(i <= 2 * chunk + 1, jnp.logical_not(kg_mine(i))))
+        @pl.when(jnp.logical_and(i <= 2 * chunk + 1, i != s))
         def _(i=i):
             kg_copy(i).wait_send()
     for d in range(1, ntp):
@@ -587,8 +582,6 @@
                 p1_copy(send, o, odd).wait_send()
     for d in range(1, ndp):
         pb_copy(d).wait_send()
-    for copy in outs:
-        copy.wait()
 
 
 def body(
@@ -617,34 +610,38 @@
         vm((tall, 128), BF16), vm((128, tall), BF16), vm((tall, 128)),
         vm((rows, wide)), vm((rows, wide)), vm((rows, wide)), vm((rows, wide)), vm((rows, wide)), vm((rows, wide)),
         vm((nheads // 2, 2 * rows, rows)), vm((nheads // 2, rows, 2 * rows), BF16),
-        vm((nheads // 2, 2 * rows, 128), BF16),
+        vm((nheads // 2, 2 * rows, 128), BF16), vm((rows, wide), BF16), vm((rows, 128)),
         vm((nseq, nheads, 128)),
         vm((wide, 128), BF16), vm((nseq, 64, 128), BF16), vm((nseq, 64, 128), BF16), vm((wide, 128), BF16),
         vm((wide, 128), BF16), vm((nseq, 64, 128), BF16), vm((nseq, 64, 128), BF16), vm((wide, 128), BF16),
         vm((2, nseq, 128, rows), BF16), vm((nseq // 2, 2, 128, rows), BF16), vm((2, nseq // 2, 128, rows), BF16),
+        vm((2, 128, rows)), vm((128, rows), BF16), vm((128, rows), BF16),
         vm((rows, 128), BF16), vm((rows, 128), BF16),
         vm((ntp, 2 * rows // ntp, 128), BF16), vm((ntp, 2 * rows // ntp, 128), BF16),
         vm((nseq, nheads, 128)), vm((ndp, nheads, 128)),
-        vm((rows, wide)), vm((64, rows)), vm((64, rows)), vm((rows, wide)), vm((rows, 128)), vm((rows, 128)),
-        vm((nheads, rows)), vm((nheads, 128)),
-        pltpu.SemaphoreType.REGULAR((4,)), dma((8,)), dma((8,)), dma((4, max(nseq // 2, 4))), dma((2, nseq)), dma((nseq,)), dma((nseq,)),
+        pltpu.SemaphoreType.REGULAR((4,)), dma((8,)), dma((4, max(nseq // 2, 4))), dma((2, nseq)), dma((nseq,)), dma((nseq,)),
         dma((nseq,)), dma((nseq,)), dma((nseq,)), dma((nseq,)),
         dma((nseq,)), dma((nseq,)), dma((nseq,)), dma((nseq,)),
-        dma((nseq // 2,)), dma((nseq // 2,)), dma((nseq,)), dma((2, nseq // 2)), dma((2, ntp)), dma((ntp,)), dma((ntp,)), dma((ntp,)),
+        dma((nseq // 2,)), dma((nseq // 2,)), dma((nseq,)), dma((2, nseq // 2)), dma(()), dma(()), dma((2, ntp)), dma((ntp,)), dma((ntp,)), dma((ntp,)),
         dma((nseq,)), dma((nseq,)), dma((ndp,)), dma((ndp,)),
     ]
     results = pl.pallas_call(
         functools.partial(kernel, dims),
-        out_shape=tuple(jax.ShapeDtypeStruct(o, F32) for o in outs),
+        out_shape=tuple(pltpu.VMEM(o, F32) for o in outs),
         in_specs=[any_spec] * 8 + [smem_spec] * 3,
-        out_specs=tuple([any_spec] * 8),
+        out_specs=tuple([pl.BlockSpec(memory_space=pltpu.VMEM)] * 8),
         scratch_shapes=scratch,
         compiler_params=pltpu.CompilerParams(
             collective_id=0, has_side_effects=True, vmem_limit_bytes=VMEM
         ),
     )(
-        query_rows, jnp.swapaxes(key_rows, 1, 2), jnp.swapaxes(value_rows, 1, 2), gate_rows, write_vec, read_vec, dt_raw,
-        out_grad, a_log, skip_gain, dt_bias,
+        *(
+            pltpu.with_memory_space_constraint(a, pltpu.HBM)
+            for a in (
+                query_rows, jnp.swapaxes(key_rows, 1, 2), jnp.swapaxes(value_rows, 1, 2), gate_rows, write_vec, read_vec,
+                dt_raw, out_grad, a_log, skip_gain, dt_bias,
+            )
+        )
     )
     per_head = jax.ShapeDtypeStruct((nheads,), F32)
     written = pl.pallas_call(
@@ -652,7 +649,7 @@
         out_shape=tuple([jax.ShapeDtypeStruct(o, F32) for o in outs[:7]] + [per_head] * 3),
         in_specs=[any_spec] * 8,
         out_specs=tuple([any_spec] * 7 + [smem_spec] * 3),
-        scratch_shapes=[dma((8,)), dma((8,)), pltpu.SMEM((nheads, 128), F32)] + [vm(o) for o in outs[:7]],
+        scratch_shapes=[dma(()), dma((8,)), pltpu.SMEM((nheads, 128), F32)],
         compiler_params=pltpu.CompilerParams(vmem_limit_bytes=VMEM),
     )(*results)
     return (
@@ -661,17 +658,13 @@
 
 
 def write_out(nheads, *refs):
-    sources, targets, (load_sem, store_sem, small), staged = refs[:8], refs[8:18], refs[18:21], refs[21:]
-    loads = [pltpu.make_async_copy(sources[7], small, load_sem.at[7])]
-    loads += [pltpu.make_async_copy(sources[i], staged[i], load_sem.at[i]) for i in range(7)]
-    for copy in loads:
+    sources, targets, (load_sem, store_sem, small) = refs[:8], refs[8:18], refs[18:]
+    load = pltpu.make_async_copy(sources[7], small, load_sem)
+    load.start()
+    stores = [pltpu.make_async_copy(a, b, store_sem.at[i]) for i, (a, b) in enumerate(zip(sources[:7], targets[:7]))]
+    for copy in stores:
         copy.start()
-    stores = []
-    for i in range(7):
-        loads[1 + i].wait()
-        stores.append(pltpu.make_async_copy(staged[i], targets[i], store_sem.at[i]))
-        stores[i].start()
-    loads[0].wait()
+    load.wait()
     for h in range(nheads):
         for i in range(3):
             targets[7 + i][h] = small[h, i]

time: 51 us -> 49.4 us (0.969)
  Pallas kernels: 50 us -> 48.5 us
    pallas_call x1, Pallas kernels: 2.49 us -> 1.47 us  [body(): pl.pallas_call(functools.partial(write_out, nheads), out_shape=tuple([jax...]
where the time goes in v5:
time: 49.4 us; the launch traced here: 49.1 us
  Pallas kernels  48.5 us (98%)
  between operations  0.65 us (1%)
    pallas_call x1, Pallas kernels, body(): pl.pallas_call(functools.partial(kernel, dims), out_shape=tuple((pltpu.VM...  47 us
    pallas_call x1, Pallas kernels, body(): pl.pallas_call(functools.partial(write_out, nheads), out_shape=tuple([jax...  1.47 us

profile of v5, /device:TPU:1, one launch (start us, length us, event | category | flops | bytes accessed | tf_op | source)
XLA Modules:
  0.0 49.1 jit_solution(14681035052188279808)
XLA Ops:
  0.6 47.0 %shard_map.186 = (f32[1,128,512]{2,1,0:T(8,128)S(1)}, f32[1,64,128]{2,1,0:T(8,128)S(1)}, f32[1,64,128]{2,1,0:T(8,128)S(1)}, f32[1,128,512]{2,1,0:T(8,128)S(1)}, ...) custom-call(bf16[1,128,512]{2,1,0:T(8,128)(2,1)} %q_hbm.1, ...), custom_call_target="tpu_custom_call" | custom-call | tf_op jit(solution)/shard_map/pallas_call | solution.py:628
  47.7 1.5 %shard_map.187 = (f32[1,128,512]{2,1,0:T(8,128)}, f32[1,64,128]{2,1,0:T(8,128)}, f32[1,64,128]{2,1,0:T(8,128)}, f32[1,128,512]{2,1,0:T(8,128)}, f32[1,128,128]{2...) custom-call(f32[1,128,512]{2,1,0:T(8,128)S(1)} %get-tuple-element.28.refs_, ...), custom_call_target="tpu_custom_call" | custom-call | tf_op jit(solution)/shard_map/pallas_call | solution.py:647

commit v6 on v5

--- a/solution.py
+++ b/solution.py
@@ -62,6 +62,8 @@
     def seq_block(ref, i, n):
         return ref.at[pl.ds(pl.multiple_of(i * n, n), n)]
 
+    far_first = sorted(range(1, nseq), key=lambda d: abs(d - nseq // 2))
+
     loads = []
     for at, (src, dst) in enumerate((
         (k_hbm.at[0], k_v), (v_hbm.at[0], v_v), (dt_hbm.at[0], dt_v), (gate_hbm.at[0], gate_v),
@@ -183,7 +185,7 @@
         def copy(d):
             to = lax.rem(s + d, nseq)
             return rcopy(seq_block(send, to, 64), recv.at[s], ss.at[d], rs.at[s], seq=to)
-        for d in range(1, nseq):
+        for d in far_first:
             copy(d).start()
         recv[s] = send[pl.ds(pl.multiple_of(s * 64, 64), 64), :]
         return copy
@@ -292,20 +294,16 @@
 
     own_head = pl.ds(pl.multiple_of(s * 64, 64), 64)
 
-    def send_back(out, recv, ss, rs, i):
-        @pl.when(s != i)
-        def _():
-            back_copy(out, recv, ss, rs, i).start()
-
-        @pl.when(s == i)
-        def _():
-            recv[own_head, :] = out[i]
+    def send_back(out, recv, ss, rs):
+        for d in far_first:
+            back_copy(out, recv, ss, rs, lax.rem(s + d, nseq)).start()
+        recv[own_head, :] = out[s]
 
     state = jnp.zeros((64, 128), F32)
     for i in reversed(range(nseq)):
         es_out[i] = state.astype(BF16)
-        send_back(es_out, ex_recv, ex_ss, ex_rs, i)
         state = es_recv[i].astype(F32) + jnp.exp(-cl_all[i, pl.ds(s, 1), :]) * state
+    send_back(es_out, ex_recv, ex_ss, ex_rs)
 
     m_buf[...] = jnp.broadcast_to(jnp.max(m_buf[...], axis=1, keepdims=True), (nq * rows, 128))
 
@@ -354,8 +352,8 @@
     state = jnp.zeros((64, 128), F32)
     for i in range(nseq):
         fs_out[i] = state.astype(BF16)
-        send_back(fs_out, fi_recv, fi_ss, fi_rs, i)
         state = fs_recv[i].astype(F32) + jnp.exp(-cl_all[i, pl.ds(s, 1), :]) * state
+    send_back(fs_out, fi_recv, fi_ss, fi_rs)
 
     wait_from(lambda j: rcopy(seq_block(ex_recv, j, 64), seq_block(ex_recv, j, 64), ex_ss.at[0], ex_rs.at[j], seq=j))
     exit_g = ex_recv[...]
@@ -367,24 +365,50 @@
     gw_send[...] = grad_w.astype(BF16)
     gr_part[...] = mm(m_sum.astype(BF16), write_v[...])
 
-    part = 2 * rows // ntp
-
-    def p1_copy(send, o, odd):
-        return rcopy(send.at[pl.ds(part * o, part)], ps_recv.at[z], p1_ss.at[odd, o], p1_rs.at[z], tp=2 * o + odd)
-
-    def p1_start(send, odd):
-        for o in range(ntp // 2):
-            @pl.when(z != 2 * o + odd)
-            def _(o=o):
-                p1_copy(send, o, odd).start()
-
-            @pl.when(z == 2 * o + odd)
-            def _(o=o):
-                ps_recv[z] = send[part * o:part * o + part, :]
+    parts = ntp // 2
+    part = rows // parts
+    mine = lax.rem(z, parts)
+
+    def p1_copy(send, kind, d):
+        to = lax.rem(z + d, ntp)
+        return rcopy(
+            seq_block(send, lax.rem(to, parts), part), ps_recv.at[kind, z], p1_ss.at[kind, d], p1_rs.at[kind, z], tp=to
+        )
+
+    def p1_start(send, kind):
+        for d in sorted(range(1, ntp), key=lambda d: abs(d - parts)):
+            p1_copy(send, kind, d).start()
+        ps_recv[kind, z] = send[pl.ds(pl.multiple_of(mine * part, part), part), :]
+
+    reach = sorted([d for d in range(-((parts - 1) // 2), parts // 2 + 1) if d], key=lambda d: -abs(d))
+
+    def p2_copy(kind, at):
+        return rcopy(
+            ps_out.at[kind, mine], ps_out.at[kind, mine], p2_ss.at[kind, at], p2_rs.at[kind, mine],
+            tp=lax.rem(z + reach[at] + ntp, ntp),
+        )
+
+    def p1_finish(kind):
+        for d in range(1, ntp):
+            j = lax.rem(z + d, ntp)
+            rcopy(ps_recv.at[kind, j], ps_recv.at[kind, j], p1_ss.at[0, 0], p1_rs.at[kind, j], tp=j).wait_recv()
+        red = ps_recv[kind, 0].astype(F32)
+        for j in range(1, ntp):
+            red = red + ps_recv[kind, j].astype(F32)
+        ps_out[kind, mine] = red.astype(BF16)
+        for at in range(len(reach)):
+            p2_copy(kind, at).start()
+
+    def p2_finish(kind, out):
+        for d in reach:
+            c = lax.rem(z - d + ntp, parts)
+            rcopy(ps_out.at[kind, c], ps_out.at[kind, c], p2_ss.at[0, 0], p2_rs.at[kind, c], tp=other).wait_recv()
+        for c in range(parts):
+            out[0, part * c:part * c + part, :] = ps_out[kind, c].astype(F32)
 
     if rounds:
         hear(len(rounds) - 1)
-    p1_start(gw_send, 1)
+    p1_start(gw_send, 0)
 
     for p in range(nq):
         r = slice(rows * p, rows * p + rows)
@@ -433,7 +457,7 @@
     entry = fi_recv[...]
     grad_r = gr_part[...] + mm(gye_b[...], entry)
     gr_send[...] = grad_r.astype(BF16)
-    p1_start(gr_send, 0)
+    p1_start(gr_send, 1)
 
     def kg_join(i, carry):
         sib_copy(i).wait()
@@ -483,22 +507,11 @@
     def pa_copy(d):
         return rcopy(pp_all.at[s], pp_all.at[s], pa_ss.at[d], pa_rs.at[s], seq=lax.rem(s + d, nseq))
 
-    for d in range(1, nseq):
+    for d in far_first:
         pa_copy(d).start()
 
-    for d in range(1, ntp):
-        j = lax.rem(z + d, ntp)
-        rcopy(ps_recv.at[j], ps_recv.at[j], p1_ss.at[0, 0], p1_rs.at[j], tp=j).wait_recv()
-    red = ps_recv[0].astype(F32)
-    for j in range(1, ntp):
-        red = red + ps_recv[j].astype(F32)
-    ps_out[z] = red.astype(BF16)
-
-    def p2_copy(d):
-        return rcopy(ps_out.at[z], ps_out.at[z], p2_ss.at[d], p2_rs.at[z], tp=lax.rem(z + d, ntp))
-
-    for d in range(1, ntp):
-        p2_copy(d).start()
+    p1_finish(0)
+    p1_finish(1)
 
     wait_from(lambda j: rcopy(pp_all.at[j], pp_all.at[j], pa_ss.at[0], pa_rs.at[j], seq=j))
     pd = pp_all[0]
@@ -539,12 +552,8 @@
         pd = pd + pd_all[j]
     pf[...] = pd
 
-    for d in range(1, ntp):
-        j = lax.rem(z + d, ntp)
-        rcopy(ps_out.at[j], ps_out.at[j], p2_ss.at[0], p2_rs.at[j], tp=j).wait_recv()
-    for o in range(ntp // 2):
-        gw_o[0, part * o:part * o + part, :] = ps_out[2 * o + 1].astype(F32)
-        gr_o[0, part * o:part * o + part, :] = ps_out[2 * o].astype(F32)
+    p2_finish(0, gw_o)
+    p2_finish(1, gr_o)
 
     for d in range(1, nchip):
         @pl.when(chunk + d < nchip)
@@ -573,13 +582,11 @@
         @pl.when(jnp.logical_and(i <= 2 * chunk + 1, i != s))
         def _(i=i):
             kg_copy(i).wait_send()
-    for d in range(1, ntp):
-        p2_copy(d).wait_send()
-    for o in range(ntp // 2):
-        for odd, send in ((1, gw_send), (0, gr_send)):
-            @pl.when(z != 2 * o + odd)
-            def _(o=o, odd=odd, send=send):
-                p1_copy(send, o, odd).wait_send()
+    for kind, send in ((0, gw_send), (1, gr_send)):
+        for d in range(1, ntp):
+            p1_copy(send, kind, d).wait_send()
+        for at in range(len(reach)):
+            p2_copy(kind, at).wait_send()
     for d in range(1, ndp):
         pb_copy(d).wait_send()
 
@@ -617,12 +624,12 @@
         vm((2, nseq, 128, rows), BF16), vm((nseq // 2, 2, 128, rows), BF16), vm((2, nseq // 2, 128, rows), BF16),
         vm((2, 128, rows)), vm((128, rows), BF16), vm((128, rows), BF16),
         vm((rows, 128), BF16), vm((rows, 128), BF16),
-        vm((ntp, 2 * rows // ntp, 128), BF16), vm((ntp, 2 * rows // ntp, 128), BF16),
+        vm((2, ntp, 2 * rows // ntp, 128), BF16), vm((2, ntp // 2, 2 * rows // ntp, 128), BF16),
         vm((nseq, nheads, 128)), vm((ndp, nheads, 128)),
         pltpu.SemaphoreType.REGULAR((4,)), dma((8,)), dma((4, max(nseq // 2, 4))), dma((2, nseq)), dma((nseq,)), dma((nseq,)),
         dma((nseq,)), dma((nseq,)), dma((nseq,)), dma((nseq,)),
         dma((nseq,)), dma((nseq,)), dma((nseq,)), dma((nseq,)),
-        dma((nseq // 2,)), dma((nseq // 2,)), dma((nseq,)), dma((2, nseq // 2)), dma(()), dma(()), dma((2, ntp)), dma((ntp,)), dma((ntp,)), dma((ntp,)),
+        dma((nseq // 2,)), dma((nseq // 2,)), dma((nseq,)), dma((2, nseq // 2)), dma(()), dma(()), dma((2, ntp)), dma((2, ntp)), dma((2, ntp)), dma((2, ntp)),
         dma((nseq,)), dma((nseq,)), dma((ndp,)), dma((ndp,)),
     ]
     results = pl.pallas_call(

time: 49.4 us -> 48.7 us (0.986)
  Pallas kernels: 48.5 us -> 47.8 us
    pallas_call x1, Pallas kernels: 47 us -> 46.3 us  [body(): pl.pallas_call(functools.partial(kernel, dims), out_shape=tuple((pltpu.VM...]
where the time goes in v6:
time: 48.7 us; the launch traced here: 48.4 us
  Pallas kernels  47.8 us (98%)
  between operations  0.65 us (1%)
    pallas_call x1, Pallas kernels, body(): pl.pallas_call(functools.partial(kernel, dims), out_shape=tuple((pltpu.VM...  46.3 us
    pallas_call x1, Pallas kernels, body(): pl.pallas_call(functools.partial(write_out, nheads), out_shape=tuple([jax...  1.47 us

profile of v6, /device:TPU:1, one launch (start us, length us, event | category | flops | bytes accessed | tf_op | source)
XLA Modules:
  0.0 48.4 jit_solution(1508790139182199374)
XLA Ops:
  0.6 46.3 %shard_map.186 = (f32[1,128,512]{2,1,0:T(8,128)S(1)}, f32[1,64,128]{2,1,0:T(8,128)S(1)}, f32[1,64,128]{2,1,0:T(8,128)S(1)}, f32[1,128,512]{2,1,0:T(8,128)S(1)}, ...) custom-call(bf16[1,128,512]{2,1,0:T(8,128)(2,1)} %q_hbm.1, ...), custom_call_target="tpu_custom_call" | custom-call | tf_op jit(solution)/shard_map/pallas_call | solution.py:635
  47.0 1.5 %shard_map.187 = (f32[1,128,512]{2,1,0:T(8,128)}, f32[1,64,128]{2,1,0:T(8,128)}, f32[1,64,128]{2,1,0:T(8,128)}, f32[1,128,512]{2,1,0:T(8,128)}, f32[1,128,128]{2...) custom-call(f32[1,128,512]{2,1,0:T(8,128)S(1)} %get-tuple-element.28.refs_, ...), custom_call_target="tpu_custom_call" | custom-call | tf_op jit(solution)/shard_map/pallas_call | solution.py:654

commit v7 on v6

--- a/solution.py
+++ b/solution.py
@@ -181,12 +181,18 @@
     gye_b[...] = gye
     es_send[...] = mm_tn(gye, read_v[...]).astype(BF16)
 
-    def all_to_all(send, recv, ss, rs):
+    def all_to_all(send, recv, ss, rs, unused=None):
         def copy(d):
             to = lax.rem(s + d, nseq)
             return rcopy(seq_block(send, to, 64), recv.at[s], ss.at[d], rs.at[s], seq=to)
-        for d in far_first:
-            copy(d).start()
+        if unused is None:
+            for d in far_first:
+                copy(d).start()
+        else:
+            @pl.when(s != unused)
+            def _():
+                for d in far_first:
+                    copy(d).start()
         recv[s] = send[pl.ds(pl.multiple_of(s * 64, 64), 64), :]
         return copy
 
@@ -328,7 +334,7 @@
 
     xw = (x_v[...] * w2x[...]).astype(BF16)
     fs_send[...] = mm_tn(xw, write_v[...]).astype(BF16)
-    fs_copy = all_to_all(fs_send, fs_recv, fs_ss, fs_rs)
+    fs_copy = all_to_all(fs_send, fs_recv, fs_ss, fs_rs, nseq - 1)
 
     m_sum = jnp.zeros((rows, rows), F32)
     col_r = jnp.zeros((nheads, rows), F32)
@@ -348,11 +354,15 @@
         row_r = jnp.where(head_i == 2 * p, rs[0:1, :rows], row_r)
         row_r = jnp.where(head_i == 2 * p + 1, rs[0:1, rows:], row_r)
 
-    wait_from(lambda j: rcopy(fs_recv.at[j], fs_recv.at[j], fs_ss.at[0], fs_rs.at[j], seq=j))
+    for j in range(nseq - 1):
+        @pl.when(s != j)
+        def _(j=j):
+            rcopy(fs_recv.at[j], fs_recv.at[j], fs_ss.at[0], fs_rs.at[j], seq=j).wait_recv()
     state = jnp.zeros((64, 128), F32)
     for i in range(nseq):
         fs_out[i] = state.astype(BF16)
-        state = fs_recv[i].astype(F32) + jnp.exp(-cl_all[i, pl.ds(s, 1), :]) * state
+        if i < nseq - 1:
+            state = fs_recv[i].astype(F32) + jnp.exp(-cl_all[i, pl.ds(s, 1), :]) * state
     send_back(fs_out, fi_recv, fi_ss, fi_rs)
 
     wait_from(lambda j: rcopy(seq_block(ex_recv, j, 64), seq_block(ex_recv, j, 64), ex_ss.at[0], ex_rs.at[j], seq=j))
@@ -571,7 +581,11 @@
     for d in range(1, nseq):
         cl_copy(d, lax.rem(s + d, nseq)).wait_send()
         es_copy(d).wait_send()
-        fs_copy(d).wait_send()
+
+        @pl.when(s != nseq - 1)
+        def _(d=d):
+            fs_copy(d).wait_send()
+
         pa_copy(d).wait_send()
     for i in range(nseq):
         @pl.when(s != i)

time: 48.7 us -> 47.7 us (0.979)
  Pallas kernels: 47.8 us -> 46.8 us
    pallas_call x1, Pallas kernels: 46.3 us -> 45.3 us  [body(): pl.pallas_call(functools.partial(kernel, dims), out_shape=tuple((pltpu.VM...]
where the time goes in v7:
time: 47.7 us; the launch traced here: 47.4 us
  Pallas kernels  46.8 us (98%)
  between operations  0.65 us (1%)
    pallas_call x1, Pallas kernels, body(): pl.pallas_call(functools.partial(kernel, dims), out_shape=tuple((pltpu.VM...  45.3 us
    pallas_call x1, Pallas kernels, body(): pl.pallas_call(functools.partial(write_out, nheads), out_shape=tuple([jax...  1.47 us

profile of v7, /device:TPU:1, one launch (start us, length us, event | category | flops | bytes accessed | tf_op | source)
XLA Modules:
  0.0 47.4 jit_solution(16777517924674737778)
XLA Ops:
  0.6 45.3 %shard_map.186 = (f32[1,128,512]{2,1,0:T(8,128)S(1)}, f32[1,64,128]{2,1,0:T(8,128)S(1)}, f32[1,64,128]{2,1,0:T(8,128)S(1)}, f32[1,128,512]{2,1,0:T(8,128)S(1)}, ...) custom-call(bf16[1,128,512]{2,1,0:T(8,128)(2,1)} %q_hbm.1, ...), custom_call_target="tpu_custom_call" | custom-call | tf_op jit(solution)/shard_map/pallas_call | solution.py:649
  46.0 1.5 %shard_map.187 = (f32[1,128,512]{2,1,0:T(8,128)}, f32[1,64,128]{2,1,0:T(8,128)}, f32[1,64,128]{2,1,0:T(8,128)}, f32[1,128,512]{2,1,0:T(8,128)}, f32[1,128,128]{2...) custom-call(f32[1,128,512]{2,1,0:T(8,128)S(1)} %get-tuple-element.28.refs_, ...), custom_call_target="tpu_custom_call" | custom-call | tf_op jit(solution)/shard_map/pallas_call | solution.py:668
